TPU v7x, 1024 devices: a whole 8x8x8 slice. The times are simulated.
1024 devices in a mesh: loop: 32 (over z_lo, x, core), grp: 32 (over z_hi, y).
Axes of the slice: x: 8, y: 8, z: 8 (z_hi: 4, z_lo: 2; z = z_hi * 2 + z_lo), core: 2. Of those that a mesh axis runs over, the one named last changes fastest.
Arguments:
- picture_features: float32 [262144, 1152], P(('loop', 'grp')), may hold values from -1.0298836 to 1.0298836
- caption_features_per_holder: float32 [131072, 1152], P(('loop', 'grp')), may hold values from -1.0298836 to 1.0298836
- dispatched_entries: int32 [32, 32, 32, 6], P('loop', 'grp'), may hold values from 0 to 127, as said below
- sent_tally: int32 [32, 32, 32], P('loop'), may hold values from 2 to 6, as said below
- positive_caption_position: int32 [262144], P(('loop', 'grp')), may hold values from 0 to 131071, as said below
- score_scale_factor: float32 [1], replicated, may hold values from 1 to 3
- score_shift_term: float32 [1], replicated, may hold values from -4 to -1
Outputs:
- image_grad: float32 [262144, 1152], P(('loop', 'grp'))
- text_grad: float32 [131072, 1152], P(('loop', 'grp'))
Inputs may be any that keep to these rules, and one draw needn't show every extreme that they name: sent_tally[l, g', g] rows go from owner (l, g') to device (l, g); every row and every column of sent_tally[l] sums to 128, and every row and every column holds an entry equal to 6. For c < sent_tally[l, g', g], dispatched_entries[l, g', g, c] names one of owner (l, g')'s owned rows; over all g and such c, each owned row is named exactly once. Later slots hold arbitrary row numbers. `positive_caption_position`: the positive text row of an image row of block (l, g) lies in text block (l - k mod 32, g) for some k < 4.
All inputs are finite; a program needn't handle non-finite values.
Results may differ from a plain program's by a relative error of at most 0.0049.
Values may be sent and summed in bfloat16 or wider, within the bound.
No kernel may reach another device: no remote copies, remote signals or barrier semaphores. Data moves between devices by JAX's collectives and lax.ppermute only.
A program may use at most 32 MiB of HBM per device.

v0:
```python
import jax
import jax.numpy as jnp
from jax import lax
from jax.sharding import PartitionSpec as P

STOPS = 4


def passed_along(value, axis, steps):
    count = lax.axis_size(axis)
    pairs = [(source, (source + steps) % count) for source in range(count)]
    return lax.ppermute(value, axis, pairs)


def slopes_for(image_part, text_part, positives, first_id, score_scaling_factor, logit_offset_bias):
    scores = lax.dot_general(
        image_part, text_part, (((1,), (1,)), ((), ())), preferred_element_type=jnp.float32
    )
    logits = score_scaling_factor * scores + logit_offset_bias
    columns = first_id + jnp.arange(text_part.shape[0], dtype=jnp.int32)
    signed = jnp.where(positives[:, None] == columns[None, :], 1.0, -1.0).astype(jnp.float32)
    return (-score_scaling_factor * signed * jax.nn.sigmoid(-signed * logits)).astype(jnp.bfloat16)


def local(
    picture_features,
    caption_features_per_holder,
    dispatched_entries,
    sent_tally,
    positive_caption_position,
    score_scale_factor,
    score_shift_term,
):
    group_count = lax.axis_size("grp")
    loop_count = lax.axis_size("loop")
    loop_at = lax.axis_index("loop")
    group_at = lax.axis_index("grp")
    block_rows, features = caption_features_per_holder.shape
    slot_cap = dispatched_entries.shape[3]
    score_scaling_factor = score_scale_factor[0]
    logit_offset_bias = score_shift_term[0]
    listed = dispatched_entries[0, 0]
    outgoing = jnp.take(
        caption_features_per_holder.astype(jnp.bfloat16), listed.reshape(-1), axis=0
    ).reshape(group_count, slot_cap, features)
    received_rows = lax.all_to_all(
        outgoing, "grp", split_axis=0, concat_axis=0, tiled=True
    ).reshape(group_count * slot_cap, features)
    incoming = lax.dynamic_index_in_dim(sent_tally[0], group_at, 1, keepdims=False)
    end_marks = jnp.cumsum(incoming)
    start_marks = end_marks - incoming
    places = jnp.arange(block_rows, dtype=jnp.int32)
    source = jnp.sum((end_marks[None, :] <= places[:, None]).astype(jnp.int32), axis=1)
    within = places - jnp.take(start_marks, source)
    text_block = jnp.take(received_rows, source * slot_cap + within, axis=0)
    image_low = picture_features.astype(jnp.bfloat16)
    image_grad = jnp.zeros(picture_features.shape, jnp.float32)
    visiting = text_block
    for stop_index in range(STOPS):
        if stop_index > 0:
            visiting = passed_along(visiting, "loop", 1)
        anchor = (loop_at - stop_index) % loop_count
        first_id = (anchor * group_count + group_at) * block_rows
        slopes = slopes_for(
            image_low,
            visiting,
            positive_caption_position,
            first_id,
            score_scaling_factor,
            logit_offset_bias,
        )
        image_grad = image_grad + jnp.dot(slopes, visiting, preferred_element_type=jnp.float32)
        partial_grad = lax.dot_general(
            slopes, image_low, (((0,), (0,)), ((), ())), preferred_element_type=jnp.float32
        )
        if stop_index == 0:
            carried = partial_grad
        else:
            carried = passed_along(carried, "loop", 1) + partial_grad
    home_grad = passed_along(carried, "loop", 1 - STOPS)
    back_places = jnp.minimum(
        start_marks[:, None] + jnp.arange(slot_cap, dtype=jnp.int32)[None, :], block_rows - 1
    )
    sendback = jnp.take(home_grad, back_places.reshape(-1), axis=0).reshape(
        group_count, slot_cap, features
    )
    returned = lax.all_to_all(sendback, "grp", split_axis=0, concat_axis=0, tiled=True)
    outgoing_counts = lax.dynamic_index_in_dim(sent_tally[0], group_at, 0, keepdims=False)
    live_slots = jnp.arange(slot_cap, dtype=jnp.int32)[None, :] < outgoing_counts[:, None]
    kept_rows = jnp.where(live_slots[:, :, None], returned, 0.0).reshape(-1, features)
    text_grad = jnp.zeros((block_rows, features), jnp.float32).at[listed.reshape(-1)].add(kept_rows)
    return (image_grad, text_grad)


def solution(mesh):
    placed = (
        P(("loop", "grp"), None),
        P(("loop", "grp"), None),
        P("loop", "grp", None, None),
        P("loop", None, None),
        P(("loop", "grp")),
        P(),
        P(),
    )
    return jax.shard_map(
        local,
        mesh=mesh,
        in_specs=placed,
        out_specs=(P(("loop", "grp"), None), P(("loop", "grp"), None)),
        check_vma=False,
    )
```

profile of v0, /device:TPU:178, one launch (start us, length us, event | category | flops | bytes accessed | tf_op | source)
XLA Modules:
  0.0 162.4 jit_solution(8562801217742676584)
XLA Ops:
  0.6 0.8 copy.19
  1.4 0.7 compare_and_fusion.1
  2.1 1.1 convert_element_type.22
  3.3 0.6 copy-done.6
  3.9 1.1 gather_fusion.1
  5.3 1.0 broadcast_select_fusion.2
  6.2 20.6 %all-to-all-start = ((bf16[32,6,1152]{2,1,0:T(8,128)(2,1)}), bf16[32,6,1152]{2,1,0:T(8,128)(2,1)S(1)}, u32[]{:S(2)}, u32[]{:S(2)}) async-start(bf16[32,6,1152]{2,1,0:T(8,128)(2,1)} %broadcast_select_fusion.2), calls=%async_computation | async-start | bytes 1179648 | tf_op jit(solution)/shard_map/all_to_all | solution.py:46
  28.7 1.2 gather_fusion
  30.0 17.1 %all-to-all-done = bf16[32,6,1152]{2,1,0:T(8,128)(2,1)S(1)} async-done(((bf16[32,6,1152]{2,1,0:T(8,128)(2,1)}), bf16[32,6,1152]{2,1,0:T(8,128)(2,1)S(1)}, u32[]{:S(2)}, u32[]{:S(2)}) %all-to-all-start) | async-done | bytes 442400 | tf_op jit(solution)/shard_map/all_to_all | solution.py:46
  47.3 0.9 gather_fusion.2
  48.4 0.4 fusion.32
  49.0 1.9 %collective-permute-start.3 = (f32[128,1152]{1,0:T(8,128)S(1)}, f32[128,1152]{1,0:T(8,128)S(1)}, u32[]{:S(2)}, u32[]{:S(2)}) collective-permute-start(f32[128,1152]{1,0:T(8,128)S(1)} %fusion.44), channel_id=1, source_target_pairs={{0,32},{32,64},{64,96},{96,128},{128,160},{160,192},{192,224},{224... | collective-permute-start | bytes 1769480 | tf_op jit(solution)/shard_map/ppermute | solution.py:12
  50.9 3.5 %collective-permute-start = (bf16[128,1152]{1,0:T(8,128)(2,1)S(1)}, bf16[128,1152]{1,0:T(8,128)(2,1)S(1)}, u32[]{:S(2)}, u32[]{:S(2)}) collective-permute-start(bf16[128,1152]{1,0:T(8,128)(2,1)S(1)} %broadcast_select_fusion.3), channel_id=1, source_target_pairs={{0,32},{32,64},{64,96},{96,128},{128,160},{160,192},{192,224},{224... | collective-permute-start | bytes 884744 | tf_op jit(solution)/shard_map/ppermute | solution.py:12
  54.5 8.9 %collective-permute-done = bf16[128,1152]{1,0:T(8,128)(2,1)S(1)} collective-permute-done((bf16[128,1152]{1,0:T(8,128)(2,1)S(1)}, bf16[128,1152]{1,0:T(8,128)(2,1)S(1)}, u32[]{:S(2)}, u32[]{:S(2)}) %collective-permute-start) | collective-permute-done | bytes 294944 | tf_op jit(solution)/shard_map/ppermute | solution.py:12
  63.4 1.9 %collective-permute-start.1 = (bf16[128,1152]{1,0:T(8,128)(2,1)S(1)}, bf16[128,1152]{1,0:T(8,128)(2,1)S(1)}, u32[]{:S(2)}, u32[]{:S(2)}) collective-permute-start(bf16[128,1152]{1,0:T(8,128)(2,1)S(1)} %collective-permute-done), channel_id=1, source_target_pairs={{0,32},{32,64},{64,96},{96,128},{128,160},{160,192},{192,224},{224... | collective-permute-start | bytes 884744 | tf_op jit(solution)/shard_map/ppermute | solution.py:12
  65.3 0.4 fusion.33
  66.0 3.5 %collective-permute-start.4 = (f32[128,1152]{1,0:T(8,128)S(1)}, f32[128,1152]{1,0:T(8,128)S(1)}, u32[]{:S(2)}, u32[]{:S(2)}) collective-permute-start(f32[128,1152]{1,0:T(8,128)S(1)} %convolution_add_fusion.3), channel_id=1, source_target_pairs={{0,32},{32,64},{64,96},{96,128},{128,160},{160,192},{192,224},{224... | collective-permute-start | bytes 1769480 | tf_op jit(solution)/shard_map/ppermute | solution.py:12
  69.5 1.9 %collective-permute-done.1 = bf16[128,1152]{1,0:T(8,128)(2,1)S(1)} collective-permute-done((bf16[128,1152]{1,0:T(8,128)(2,1)S(1)}, bf16[128,1152]{1,0:T(8,128)(2,1)S(1)}, u32[]{:S(2)}, u32[]{:S(2)}) %collective-permute-start.1) | collective-permute-done | bytes 294944 | tf_op jit(solution)/shard_map/ppermute | solution.py:12
  71.4 1.9 %collective-permute-start.2 = (bf16[128,1152]{1,0:T(8,128)(2,1)S(1)}, bf16[128,1152]{1,0:T(8,128)(2,1)S(1)}, u32[]{:S(2)}, u32[]{:S(2)}) collective-permute-start(bf16[128,1152]{1,0:T(8,128)(2,1)S(1)} %collective-permute-done.1), channel_id=1, source_target_pairs={{0,32},{32,64},{64,96},{96,128},{128,160},{160,192},{192,224},{224... | collective-permute-start | bytes 884744 | tf_op jit(solution)/shard_map/ppermute | solution.py:12
  74.0 3.8 %collective-permute-done.4 = f32[128,1152]{1,0:T(8,128)S(1)} collective-permute-done((f32[128,1152]{1,0:T(8,128)S(1)}, f32[128,1152]{1,0:T(8,128)S(1)}, u32[]{:S(2)}, u32[]{:S(2)}) %collective-permute-start.4) | collective-permute-done | bytes 589856 | tf_op jit(solution)/shard_map/ppermute | solution.py:12
  77.8 1.9 %collective-permute-start.5 = (f32[128,1152]{1,0:T(8,128)S(1)}, f32[128,1152]{1,0:T(8,128)S(1)}, u32[]{:S(2)}, u32[]{:S(2)}) collective-permute-start(f32[128,1152]{1,0:T(8,128)S(1)} %add.314), channel_id=1, source_target_pairs={{0,32},{32,64},{64,96},{96,128},{128,160},{160,192},{192,224},{224... | collective-permute-start | bytes 1769480 | tf_op jit(solution)/shard_map/ppermute | solution.py:12
  79.7 1.2 collective-permute-done.2
  81.5 7.5 %collective-permute-done.5 = f32[128,1152]{1,0:T(8,128)S(1)} collective-permute-done((f32[128,1152]{1,0:T(8,128)S(1)}, f32[128,1152]{1,0:T(8,128)S(1)}, u32[]{:S(2)}, u32[]{:S(2)}) %collective-permute-start.5) | collective-permute-done | bytes 589856 | tf_op jit(solution)/shard_map/ppermute | solution.py:12
  89.0 7.5 %collective-permute-start.6 = (f32[128,1152]{1,0:T(8,128)S(1)}, f32[128,1152]{1,0:T(8,128)S(1)}, u32[]{:S(2)}, u32[]{:S(2)}) collective-permute-start(f32[128,1152]{1,0:T(8,128)S(1)} %add.315), channel_id=1, source_target_pairs={{0,928},{32,960},{64,992},{96,0},{128,32},{160,64},{192,96},{224,1... | collective-permute-start | bytes 1769480 | tf_op jit(solution)/shard_map/ppermute | solution.py:12
  96.9 18.3 %collective-permute-done.6 = f32[128,1152]{1,0:T(8,128)S(1)} collective-permute-done((f32[128,1152]{1,0:T(8,128)S(1)}, f32[128,1152]{1,0:T(8,128)S(1)}, u32[]{:S(2)}, u32[]{:S(2)}) %collective-permute-start.6) | collective-permute-done | bytes 589856 | tf_op jit(solution)/shard_map/ppermute | solution.py:12
  115.2 1.0 gather_fusion.3
  116.3 1.2 broadcast_select_fusion.1
  117.5 5.7 %all-to-all-start.1 = ((f32[32,6,1152]{2,1,0:T(8,128)}), f32[32,6,1152]{2,1,0:T(8,128)S(1)}, u32[]{:S(2)}, u32[]{:S(2)}) async-start(f32[32,6,1152]{2,1,0:T(8,128)} %broadcast_select_fusion.1), calls=%async_computation.1 | async-start | bytes 2359296 | tf_op jit(solution)/shard_map/all_to_all | solution.py:87
  123.7 0.4 copy-done.4
  124.8 1.4 convolution_add_fusion
  126.1 32.7 %all-to-all-done.1 = f32[32,6,1152]{2,1,0:T(8,128)S(1)} async-done(((f32[32,6,1152]{2,1,0:T(8,128)}), f32[32,6,1152]{2,1,0:T(8,128)S(1)}, u32[]{:S(2)}, u32[]{:S(2)}) %all-to-all-start.1) | async-done | bytes 884768 | tf_op jit(solution)/shard_map/all_to_all | solution.py:87
  159.1 3.3 %scatter_custom_fusion = f32[128,1152]{1,0:T(8,128)} fusion(s32[192]{0:T(256)} %bitcast.131, f32[192,1152]{1,0:T(8,128)S(1)} %reshape.279, f32[]{:T(128)} %constant.122.clone.1), kind=kCustom, calls=%fused_computation.52 | custom fusion | flops 221184 | bytes 590336 | tf_op jit(solution)/shard_map/scatter-add | solution.py:91
  (60 shorter events, 4.9 us)
Async XLA Ops:
  3.3 0.6 copy-start.6
  5.2 21.6 %copy-start.5 = (s32[1,32,32]{2,1,0:T(8,128)S(1)}, s32[1,32,32]{2,1,0:T(8,128)}, u32[]{:S(2)}) copy-start(s32[1,32,32]{2,1,0:T(8,128)} %param.10) | copy-start | bytes 12292
  5.2 22.1 %copy-start = (f32[256,1152]{1,0:T(8,128)S(1)}, f32[256,1152]{1,0:T(8,128)}, u32[]{:S(2)}) copy-start(f32[256,1152]{1,0:T(8,128)} %param.7) | copy-start | bytes 3538948
  6.2 40.9 %all-to-all-start = ((bf16[32,6,1152]{2,1,0:T(8,128)(2,1)}), bf16[32,6,1152]{2,1,0:T(8,128)(2,1)S(1)}, u32[]{:S(2)}, u32[]{:S(2)}) async-start(bf16[32,6,1152]{2,1,0:T(8,128)(2,1)} %broadcast_select_fusion.2), calls=%async_computation | async-start | bytes 1179648 | tf_op jit(solution)/shard_map/all_to_all | solution.py:46
  47.3 1.0 copy-start.7
  48.7 16.9 %copy-start.1 = (bf16[256,128]{0,1:T(8,128)(2,1)}, bf16[256,128]{0,1:T(8,128)(2,1)S(1)}, u32[]{:S(2)}) copy-start(bf16[256,128]{0,1:T(8,128)(2,1)S(1)} %fusion.32) | copy-start | bytes 196612
  49.0 16.7 %collective-permute-start.3 = (f32[128,1152]{1,0:T(8,128)S(1)}, f32[128,1152]{1,0:T(8,128)S(1)}, u32[]{:S(2)}, u32[]{:S(2)}) collective-permute-start(f32[128,1152]{1,0:T(8,128)S(1)} %fusion.44), channel_id=1, source_target_pairs={{0,32},{32,64},{64,96},{96,128},{128,160},{160,192},{192,224},{224... | collective-permute-start | bytes 1769480 | tf_op jit(solution)/shard_map/ppermute | solution.py:12
  50.9 12.4 %collective-permute-start = (bf16[128,1152]{1,0:T(8,128)(2,1)S(1)}, bf16[128,1152]{1,0:T(8,128)(2,1)S(1)}, u32[]{:S(2)}, u32[]{:S(2)}) collective-permute-start(bf16[128,1152]{1,0:T(8,128)(2,1)S(1)} %broadcast_select_fusion.3), channel_id=1, source_target_pairs={{0,32},{32,64},{64,96},{96,128},{128,160},{160,192},{192,224},{224... | collective-permute-start | bytes 884744 | tf_op jit(solution)/shard_map/ppermute | solution.py:12
  63.4 8.0 %collective-permute-start.1 = (bf16[128,1152]{1,0:T(8,128)(2,1)S(1)}, bf16[128,1152]{1,0:T(8,128)(2,1)S(1)}, u32[]{:S(2)}, u32[]{:S(2)}) collective-permute-start(bf16[128,1152]{1,0:T(8,128)(2,1)S(1)} %collective-permute-done), channel_id=1, source_target_pairs={{0,32},{32,64},{64,96},{96,128},{128,160},{160,192},{192,224},{224... | collective-permute-start | bytes 884744 | tf_op jit(solution)/shard_map/ppermute | solution.py:12
  65.7 8.0 %copy-start.3 = (bf16[256,128]{0,1:T(8,128)(2,1)}, bf16[256,128]{0,1:T(8,128)(2,1)S(1)}, u32[]{:S(2)}) copy-start(bf16[256,128]{0,1:T(8,128)(2,1)S(1)} %fusion.33) | copy-start | bytes 196612
  66.0 11.8 %collective-permute-start.4 = (f32[128,1152]{1,0:T(8,128)S(1)}, f32[128,1152]{1,0:T(8,128)S(1)}, u32[]{:S(2)}, u32[]{:S(2)}) collective-permute-start(f32[128,1152]{1,0:T(8,128)S(1)} %convolution_add_fusion.3), channel_id=1, source_target_pairs={{0,32},{32,64},{64,96},{96,128},{128,160},{160,192},{192,224},{224... | collective-permute-start | bytes 1769480 | tf_op jit(solution)/shard_map/ppermute | solution.py:12
  71.4 9.5 %collective-permute-start.2 = (bf16[128,1152]{1,0:T(8,128)(2,1)S(1)}, bf16[128,1152]{1,0:T(8,128)(2,1)S(1)}, u32[]{:S(2)}, u32[]{:S(2)}) collective-permute-start(bf16[128,1152]{1,0:T(8,128)(2,1)S(1)} %collective-permute-done.1), channel_id=1, source_target_pairs={{0,32},{32,64},{64,96},{96,128},{128,160},{160,192},{192,224},{224... | collective-permute-start | bytes 884744 | tf_op jit(solution)/shard_map/ppermute | solution.py:12
  77.8 11.2 %collective-permute-start.5 = (f32[128,1152]{1,0:T(8,128)S(1)}, f32[128,1152]{1,0:T(8,128)S(1)}, u32[]{:S(2)}, u32[]{:S(2)}) collective-permute-start(f32[128,1152]{1,0:T(8,128)S(1)} %add.314), channel_id=1, source_target_pairs={{0,32},{32,64},{64,96},{96,128},{128,160},{160,192},{192,224},{224... | collective-permute-start | bytes 1769480 | tf_op jit(solution)/shard_map/ppermute | solution.py:12
  89.0 26.1 %collective-permute-start.6 = (f32[128,1152]{1,0:T(8,128)S(1)}, f32[128,1152]{1,0:T(8,128)S(1)}, u32[]{:S(2)}, u32[]{:S(2)}) collective-permute-start(f32[128,1152]{1,0:T(8,128)S(1)} %add.315), channel_id=1, source_target_pairs={{0,928},{32,960},{64,992},{96,0},{128,32},{160,64},{192,96},{224,1... | collective-permute-start | bytes 1769480 | tf_op jit(solution)/shard_map/ppermute | solution.py:12
  117.5 5.8 %copy-start.2 = (bf16[256,128]{0,1:T(8,128)(2,1)S(1)}, bf16[256,128]{0,1:T(8,128)(2,1)}, u32[]{:S(2)}) copy-start(bf16[256,128]{0,1:T(8,128)(2,1)} %copy-done.1) | copy-start | bytes 196612
  117.5 41.3 %all-to-all-start.1 = ((f32[32,6,1152]{2,1,0:T(8,128)}), f32[32,6,1152]{2,1,0:T(8,128)S(1)}, u32[]{:S(2)}, u32[]{:S(2)}) async-start(f32[32,6,1152]{2,1,0:T(8,128)} %broadcast_select_fusion.1), calls=%async_computation.1 | async-start | bytes 2359296 | tf_op jit(solution)/shard_map/all_to_all | solution.py:87
  123.2 0.8 copy-start.4
where the time goes:
time: 163 us; the launch traced here: 162 us
  waiting for transfers between devices  91.2 us (56%)
  starting transfers between devices  48.4 us (30%)
  other arithmetic  8.08 us (5%)
  local copies, waits for them, and re-layouts  7.26 us (4%)
  matrix products  4.91 us (3%)
  between operations  2.45 us (2%)
    ppermute x7, waiting for transfers between devices, passed_along(): return lax.ppermute(value, axis, pairs)  41.5 us
    all_to_all x1, waiting for transfers between devices, local(): lax.all_to_all(sendback, 'grp', split_axis=0, concat_axis=0, tiled=True)  32.7 us
    ppermute x7, starting transfers between devices, passed_along(): return lax.ppermute(value, axis, pairs)  22.1 us
    all_to_all x1, starting transfers between devices, local(): lax.all_to_all(outgoing, 'grp', split_axis=0, concat_axis=0, tiled=True)  20.6 us
    all_to_all x1, waiting for transfers between devices, local(): lax.all_to_all(outgoing, 'grp', split_axis=0, concat_axis=0, tiled=True)  17.1 us
    all_to_all x1, starting transfers between devices, local(): lax.all_to_all(sendback, 'grp', split_axis=0, concat_axis=0, tiled=True)  5.68 us
  transfers between devices with their start and end apart: 9, of which 8 were waited for; matrix products, arithmetic and copies ran while one was open for 4% of the time, Pallas kernels for 0%

commit v1 on v0

v1 whole, which is shorter than its diff:
```python
import jax
import jax.numpy as jnp
from jax import lax
from jax.experimental import pallas as pl
from jax.experimental.pallas import tpu as pltpu
from jax.sharding import PartitionSpec as P

STOPS = 4
LANES = 128
AUX_ROWS = 16
BF16 = jnp.bfloat16
F32 = jnp.float32


def passed_along(value, axis, steps):
    count = lax.axis_size(axis)
    pairs = [(source, (source + steps) % count) for source in range(count)]
    return lax.ppermute(value, axis, pairs)


def iota(shape, dim):
    return lax.broadcasted_iota(jnp.int32, shape, dim)


def rows_to_chunks(rows, staging, chunks_ref):
    peers, chunk_rows, _ = chunks_ref.shape
    pitch = staging.shape[0] // peers
    tiles = rows.shape[1] // LANES
    for slot in range(rows.shape[0] // peers):
        for tile in range(tiles):
            staging[pl.ds(slot * tiles + tile, peers, stride=pitch), :] = rows[
                slot * peers : (slot + 1) * peers, tile * LANES : (tile + 1) * LANES
            ]
    for peer in range(peers):
        chunks_ref[peer] = staging[peer * pitch : peer * pitch + chunk_rows, :].astype(chunks_ref.dtype)


def chunks_to_rows(chunks_ref, staging, rows_ref):
    peers, chunk_rows, _ = chunks_ref.shape
    pitch = staging.shape[0] // peers
    tiles = rows_ref.shape[1] // LANES
    for peer in range(peers):
        staging[peer * pitch : peer * pitch + chunk_rows, :] = chunks_ref[peer].astype(F32)
    for slot in range(rows_ref.shape[0] // peers):
        for tile in range(tiles):
            rows_ref[slot * peers : (slot + 1) * peers, tile * LANES : (tile + 1) * LANES] = staging[
                pl.ds(slot * tiles + tile, peers, stride=pitch), :
            ].astype(rows_ref.dtype)


def hits(columns, width):
    return jnp.concatenate(
        [(column == iota((column.shape[0], width), 1)).astype(F32) for column in columns], axis=0
    ).astype(BF16)


def block_places(tally, group_at, slot_cap, width):
    peers = tally.shape[0]
    mine = jnp.where(iota(tally.shape, 1) == group_at, tally, 0)
    before = (iota((peers, peers), 1) < iota((peers, peers), 0)).astype(F32)
    starts = jnp.dot(before, mine.astype(F32), preferred_element_type=F32)
    incoming = jnp.sum(mine, axis=1, keepdims=True)
    first = jnp.sum(starts, axis=1, keepdims=True).astype(jnp.int32)
    return hits([jnp.where(incoming > slot, first + slot, -1) for slot in range(slot_cap)], width)


def slopes_for(text, image, places, scale, shift):
    scores = lax.dot_general(text, image, (((1,), (1,)), ((), ())), preferred_element_type=F32)
    logits = scale * scores + shift
    positive = places == iota(scores.shape, 0)
    toward = jax.nn.sigmoid(jnp.where(positive, -logits, logits))
    return (jnp.where(positive, -scale, scale) * toward).astype(BF16)


def picture_kernel(loop_count, group_count, text_rows, picture_ref, positive_ref, packet_ref):
    rows = picture_ref.shape[0]
    packet_ref[0:rows, :] = picture_ref[...].astype(BF16)
    positive = positive_ref[...]
    anchor = positive // (group_count * text_rows)
    behind = lax.rem(lax.axis_index("loop") - anchor + loop_count, loop_count)
    place = lax.rem(positive, text_rows)
    packet_ref[rows:, :] = jnp.zeros((AUX_ROWS, packet_ref.shape[1]), BF16)
    packet_ref[rows:, 0:rows] = jnp.where(behind == iota((AUX_ROWS, rows), 0), place, -1).astype(F32).astype(BF16)


def dispatch_kernel(caption_ref, listed_ref, chunks_ref, staging):
    listed = listed_ref[0, 0]
    chosen = hits([listed[:, slot : slot + 1] for slot in range(listed.shape[1])], caption_ref.shape[0])
    rows = jnp.dot(chosen, caption_ref[...].astype(BF16), preferred_element_type=F32)
    rows_to_chunks(rows, staging, chunks_ref)


def assemble_kernel(chunks_ref, tally_ref, block_ref, staging, rows_ref):
    slot_cap = rows_ref.shape[0] // chunks_ref.shape[0]
    chunks_to_rows(chunks_ref, staging, rows_ref)
    places = block_places(tally_ref[0], lax.axis_index("grp"), slot_cap, block_ref.shape[0])
    block_ref[...] = lax.dot_general(
        places, rows_ref[...], (((0,), (0,)), ((), ())), preferred_element_type=F32
    ).astype(BF16)


def text_kernel(scale_ref, shift_ref, tally_ref, block_ref, *refs):
    packets, chunks_ref, staging = refs[:STOPS], refs[STOPS], refs[STOPS + 1]
    scale, shift = scale_ref[0], shift_ref[0]
    text = block_ref[...]
    rows = packets[0].shape[0] - AUX_ROWS
    total = jnp.zeros(text.shape, F32)
    for stop, packet in enumerate(packets):
        image = packet[0:rows, :]
        places = packet[rows:, 0:rows].astype(F32)[stop : stop + 1, :].astype(jnp.int32)
        total = total + jnp.dot(slopes_for(text, image, places, scale, shift), image, preferred_element_type=F32)
    slot_cap = chunks_ref.shape[1] * LANES // text.shape[1]
    slots = block_places(tally_ref[0], lax.axis_index("grp"), slot_cap, text.shape[0])
    rows_to_chunks(jnp.dot(slots, total.astype(BF16), preferred_element_type=F32), staging, chunks_ref)


def image_kernel(scale_ref, shift_ref, packet_ref, *refs):
    blocks, grad_ref = refs[:STOPS], refs[STOPS]
    scale, shift = scale_ref[0], shift_ref[0]
    rows = grad_ref.shape[0]
    image = packet_ref[0:rows, :]
    aux = packet_ref[rows:, 0:rows].astype(F32)
    slopes = [
        slopes_for(block[...], image, aux[stop : stop + 1, :].astype(jnp.int32), scale, shift)
        for stop, block in enumerate(blocks)
    ]
    width = 3 * LANES
    for start in range(0, grad_ref.shape[1], width):
        total = None
        for slope, block in zip(slopes, blocks):
            part = lax.dot_general(
                slope, block[:, start : start + width], (((0,), (0,)), ((), ())), preferred_element_type=F32
            )
            total = part if total is None else total + part
        grad_ref[:, start : start + width] = total


def return_kernel(chunks_ref, listed_ref, tally_ref, grad_ref, staging, rows_ref):
    chunks_to_rows(chunks_ref, staging, rows_ref)
    listed, tally = listed_ref[0, 0], tally_ref[0]
    peers, slot_cap = listed.shape
    mine = jnp.sum(jnp.where(iota(tally.shape, 0) == lax.axis_index("grp"), tally, 0), axis=0, keepdims=True)
    upright = iota((peers, peers), 0) == iota((peers, peers), 1)
    outgoing = jnp.sum(jnp.where(upright, mine, 0), axis=1, keepdims=True)
    owned = hits(
        [jnp.where(outgoing > slot, listed[:, slot : slot + 1], -1) for slot in range(slot_cap)], grad_ref.shape[0]
    )
    grad_ref[...] = lax.dot_general(owned, rows_ref[...], (((0,), (0,)), ((), ())), preferred_element_type=F32)


def local(
    picture_features,
    caption_features_per_holder,
    dispatched_entries,
    sent_tally,
    positive_caption_position,
    score_scale_factor,
    score_shift_term,
):
    group_count = lax.axis_size("grp")
    loop_count = lax.axis_size("loop")
    image_rows, features = picture_features.shape
    text_rows = caption_features_per_holder.shape[0]
    slot_cap = dispatched_entries.shape[3]
    chunk_rows = slot_cap * features // LANES
    pitch = -(-chunk_rows // 8) * 8

    whole = pl.BlockSpec(memory_space=pltpu.VMEM)
    scalar = pl.BlockSpec(memory_space=pltpu.SMEM)
    params = pltpu.CompilerParams(vmem_limit_bytes=48 * 1024 * 1024)
    staging = pltpu.VMEM((group_count * pitch, LANES), F32)
    slot_rows = pltpu.VMEM((group_count * slot_cap, features), BF16)
    chunks = jax.ShapeDtypeStruct((group_count, chunk_rows, LANES), BF16)

    def call(kernel, in_specs, out_shape, scratch=()):
        return pl.pallas_call(
            kernel,
            out_shape=out_shape,
            in_specs=in_specs,
            out_specs=whole,
            scratch_shapes=list(scratch),
            compiler_params=params,
        )

    def picture_body(*refs):
        picture_kernel(loop_count, group_count, text_rows, *refs)

    packet = call(
        picture_body, [whole] * 2, jax.ShapeDtypeStruct((image_rows + AUX_ROWS, features), BF16)
    )(picture_features, positive_caption_position.reshape(1, -1))
    packet_two = passed_along(packet, "loop", -2)
    packet_one = passed_along(packet, "loop", -1)
    packet_three = passed_along(packet_two, "loop", -1)

    outgoing = call(dispatch_kernel, [whole] * 2, chunks, [staging])(caption_features_per_holder, dispatched_entries)
    incoming = lax.all_to_all(outgoing, "grp", split_axis=0, concat_axis=0, tiled=True)
    block = call(
        assemble_kernel, [whole] * 2, jax.ShapeDtypeStruct((text_rows, features), BF16), [staging, slot_rows]
    )(incoming, sent_tally)

    sendback = call(text_kernel, [scalar] * 2 + [whole] * (2 + STOPS), chunks, [staging])(
        score_scale_factor, score_shift_term, sent_tally, block, packet, packet_one, packet_two, packet_three
    )
    returned = lax.all_to_all(sendback, "grp", split_axis=0, concat_axis=0, tiled=True)

    block_two = passed_along(block, "loop", 2)
    block_one = passed_along(block, "loop", 1)
    block_three = passed_along(block_two, "loop", 1)
    image_grad = call(
        image_kernel, [scalar] * 2 + [whole] * (1 + STOPS), jax.ShapeDtypeStruct((image_rows, features), F32)
    )(score_scale_factor, score_shift_term, packet, block, block_one, block_two, block_three)

    text_grad = call(
        return_kernel, [whole] * 3, jax.ShapeDtypeStruct((text_rows, features), F32), [staging, slot_rows]
    )(returned, dispatched_entries, sent_tally)
    return (image_grad, text_grad)


def solution(mesh):
    placed = (
        P(("loop", "grp"), None),
        P(("loop", "grp"), None),
        P("loop", "grp", None, None),
        P("loop", None, None),
        P(("loop", "grp")),
        P(),
        P(),
    )
    return jax.shard_map(
        local,
        mesh=mesh,
        in_specs=placed,
        out_specs=(P(("loop", "grp"), None), P(("loop", "grp"), None)),
        check_vma=False,
    )
```

time: 163 us -> 102 us (0.63)
  the two profiles are of different devices: /device:TPU:178 before, /device:TPU:16 now
where the time goes in v1:
time: 102 us; the launch traced here: 101 us
  starting transfers between devices  52.5 us (51%)
  waiting for transfers between devices  35.7 us (35%)
  Pallas kernels  9.03 us (9%)
  between operations  2.05 us (2%)
  local copies, waits for them, and re-layouts  2.04 us (2%)
    ppermute x6, waiting for transfers between devices, passed_along(): return lax.ppermute(value, axis, pairs)  23.9 us
    all_to_all x1, starting transfers between devices, local(): lax.all_to_all(outgoing, 'grp', split_axis=0, concat_axis=0, tiled=True)  21.1 us
    ppermute x6, starting transfers between devices, passed_along(): return lax.ppermute(value, axis, pairs)  18.8 us
    all_to_all x1, starting transfers between devices, local(): lax.all_to_all(sendback, 'grp', split_axis=0, concat_axis=0, tiled=True)  12.7 us
    all_to_all x1, waiting for transfers between devices, local(): lax.all_to_all(outgoing, 'grp', split_axis=0, concat_axis=0, tiled=True)  11.8 us
    pallas_call x1, Pallas kernels, local(): call(text_kernel, [scalar] * 2 + [whole] * (2 + STOPS), chunks, [staging])  3.18 us
    pallas_call x1, Pallas kernels, local(): call(image_kernel, [scalar] * 2 + [whole] * (1 + STOPS), jax.ShapeDtypeSt...  2.62 us
    unnamed x11, local copies, waits for them, and re-layouts  2.04 us
  transfers between devices with their start and end apart: 8, of which 4 were waited for; matrix products, arithmetic and copies ran while one was open for 0% of the time, Pallas kernels for 4%

profile of v1, /device:TPU:16, one launch (start us, length us, event | category | flops | bytes accessed | tf_op | source)
XLA Modules:
  0.0 101.4 jit_solution(14050241265129926407)
XLA Ops:
  0.6 0.0 copy-start
  0.6 1.3 %copy-done = f32[256,1152]{1,0:T(8,128)S(1)} copy-done((f32[256,1152]{1,0:T(8,128)S(1)}, f32[256,1152]{1,0:T(8,128)}, u32[]{:S(2)}) %copy-start) | copy-done | bytes 1179672
  1.9 0.0 copy-start.3
  1.9 0.7 copy-done.3
  2.6 0.0 copy-start.4
  2.6 0.0 copy-start.1
  2.6 0.1 shard_map.86.packet_ref.refs_0_
  2.7 7.6 %collective-permute-start.4 = (bf16[272,1152]{1,0:T(8,128)(2,1)S(1)}, bf16[272,1152]{1,0:T(8,128)(2,1)S(1)}, u32[]{:S(2)}, u32[]{:S(2)}) collective-permute-start(bf16[272,1152]{1,0:T(8,128)(2,1)S(1)} %shard_map.86.packet_ref.refs_0_), channel_id=1, source_target_pairs={{0,960},{32,992},{64,0},{96,32},{128,64},{160,96},{192,128},{224,1... | collective-permute-start | bytes 1880072 | tf_op jit(solution)/shard_map/ppermute | solution.py:18
  10.3 0.0 copy-done.4
  10.3 0.1 copy.9.listed_ref
  10.4 0.0 copy-done.1
  10.4 1.2 %shard_map.87 = bf16[32,54,128]{2,1,0:T(8,128)(2,1)} custom-call(f32[128,1152]{1,0:T(8,128)S(1)} %copy-done.1, s32[1,1,32,6]{3,2,1,0:T(8,128)S(1)} %copy.9.listed_ref), custom_call_target="tpu_custom_call" | custom-call | tf_op jit(solution)/shard_map/pallas_call | solution.py:195
  11.6 21.1 %all-to-all-start = ((bf16[32,54,128]{2,1,0:T(8,128)(2,1)}), bf16[32,54,128]{2,1,0:T(8,128)(2,1)S(1)}, u32[]{:S(2)}, u32[]{:S(2)}) async-start(bf16[32,54,128]{2,1,0:T(8,128)(2,1)} %shard_map.87), calls=%async_computation | async-start | bytes 917504 | tf_op jit(solution)/shard_map/all_to_all | solution.py:196
  32.7 2.0 %collective-permute-start.3 = (bf16[272,1152]{1,0:T(8,128)(2,1)S(1)}, bf16[272,1152]{1,0:T(8,128)(2,1)S(1)}, u32[]{:S(2)}, u32[]{:S(2)}) collective-permute-start(bf16[272,1152]{1,0:T(8,128)(2,1)S(1)} %shard_map.86.packet_ref.refs_0_), channel_id=1, source_target_pairs={{0,992},{32,0},{64,32},{96,64},{128,96},{160,128},{192,160},{224,1... | collective-permute-start | bytes 1880072 | tf_op jit(solution)/shard_map/ppermute | solution.py:18
  34.7 0.0 collective-permute-done.4.refs_2_
  34.7 3.4 %collective-permute-start.5 = (bf16[272,1152]{1,0:T(8,128)(2,1)S(1)}, bf16[272,1152]{1,0:T(8,128)(2,1)S(1)}, u32[]{:S(2)}, u32[]{:S(2)}) collective-permute-start(bf16[272,1152]{1,0:T(8,128)(2,1)S(1)} %collective-permute-done.4.refs_2_), channel_id=1, source_target_pairs={{0,992},{32,0},{64,32},{96,64},{128,96},{160,128},{192,160},{224,1... | collective-permute-start | bytes 1880072 | tf_op jit(solution)/shard_map/ppermute | solution.py:18
  39.4 11.8 %all-to-all-done.chunks_ref = bf16[32,54,128]{2,1,0:T(8,128)(2,1)S(1)} async-done(((bf16[32,54,128]{2,1,0:T(8,128)(2,1)}), bf16[32,54,128]{2,1,0:T(8,128)(2,1)S(1)}, u32[]{:S(2)}, u32[]{:S(2)}) %all-to-all-start) | async-done | bytes 442400 | tf_op jit(solution)/shard_map/all_to_all | solution.py:196
  51.2 0.0 copy-done.2
  51.2 0.6 shard_map.88.refs_0_.block_ref
  51.8 0.0 collective-permute-done.3.refs_1_
  51.8 2.7 %collective-permute-done.5.refs_3_ = bf16[272,1152]{1,0:T(8,128)(2,1)S(1)} collective-permute-done((bf16[272,1152]{1,0:T(8,128)(2,1)S(1)}, bf16[272,1152]{1,0:T(8,128)(2,1)S(1)}, u32[]{:S(2)}, u32[]{:S(2)}) %collective-permute-start.5) | collective-permute-done | bytes 626720 | tf_op jit(solution)/shard_map/ppermute | solution.py:18
  54.5 3.2 %shard_map.90 = bf16[32,54,128]{2,1,0:T(8,128)(2,1)} custom-call(f32[1]{0:T(128)S(6)} %copy.11.scale_ref, f32[1]{0:T(128)S(6)} %copy.12.shift_ref, s32[1,32,32]{2,1,0:T(8,128)S(1)} %copy-done.2, bf16[128,1152]{1,0:T(8,128)(2,1)S(1)} %shard_map.88.refs_0_.block_ref, bf16[272,1152]{1,0:T(8,128)(2,1)S(1)} %shard_map.86.packet_ref.refs_0_, ...), custom_call_target="tpu_custom_call" | custom-call | tf_op jit(solution)/shard_map/pallas_call | solution.py:201
  57.7 12.7 %all-to-all-start.1 = ((bf16[32,54,128]{2,1,0:T(8,128)(2,1)}), bf16[32,54,128]{2,1,0:T(8,128)(2,1)S(1)}, u32[]{:S(2)}, u32[]{:S(2)}) async-start(bf16[32,54,128]{2,1,0:T(8,128)(2,1)} %shard_map.90), calls=%async_computation.1 | async-start | bytes 917504 | tf_op jit(solution)/shard_map/all_to_all | solution.py:204
  70.3 1.9 %collective-permute-start.1 = (bf16[128,1152]{1,0:T(8,128)(2,1)S(1)}, bf16[128,1152]{1,0:T(8,128)(2,1)S(1)}, u32[]{:S(2)}, u32[]{:S(2)}) collective-permute-start(bf16[128,1152]{1,0:T(8,128)(2,1)S(1)} %shard_map.88.refs_0_.block_ref), channel_id=1, source_target_pairs={{0,64},{32,96},{64,128},{96,160},{128,192},{160,224},{192,256},{22... | collective-permute-start | bytes 884744 | tf_op jit(solution)/shard_map/ppermute | solution.py:18
  72.3 1.9 %collective-permute-start = (bf16[128,1152]{1,0:T(8,128)(2,1)S(1)}, bf16[128,1152]{1,0:T(8,128)(2,1)S(1)}, u32[]{:S(2)}, u32[]{:S(2)}) collective-permute-start(bf16[128,1152]{1,0:T(8,128)(2,1)S(1)} %shard_map.88.refs_0_.block_ref), channel_id=1, source_target_pairs={{0,32},{32,64},{64,96},{96,128},{128,160},{160,192},{192,224},{224... | collective-permute-start | bytes 884744 | tf_op jit(solution)/shard_map/ppermute | solution.py:18
  74.2 13.0 %collective-permute-done.1.refs_2_ = bf16[128,1152]{1,0:T(8,128)(2,1)S(1)} collective-permute-done((bf16[128,1152]{1,0:T(8,128)(2,1)S(1)}, bf16[128,1152]{1,0:T(8,128)(2,1)S(1)}, u32[]{:S(2)}, u32[]{:S(2)}) %collective-permute-start.1) | collective-permute-done | bytes 294944 | tf_op jit(solution)/shard_map/ppermute | solution.py:18
  87.2 1.9 %collective-permute-start.2 = (bf16[128,1152]{1,0:T(8,128)(2,1)S(1)}, bf16[128,1152]{1,0:T(8,128)(2,1)S(1)}, u32[]{:S(2)}, u32[]{:S(2)}) collective-permute-start(bf16[128,1152]{1,0:T(8,128)(2,1)S(1)} %collective-permute-done.1.refs_2_), channel_id=1, source_target_pairs={{0,32},{32,64},{64,96},{96,128},{128,160},{160,192},{192,224},{224... | collective-permute-start | bytes 884744 | tf_op jit(solution)/shard_map/ppermute | solution.py:18
  89.2 0.0 collective-permute-done.refs_1_
  89.2 8.2 %collective-permute-done.2.refs_3_ = bf16[128,1152]{1,0:T(8,128)(2,1)S(1)} collective-permute-done((bf16[128,1152]{1,0:T(8,128)(2,1)S(1)}, bf16[128,1152]{1,0:T(8,128)(2,1)S(1)}, u32[]{:S(2)}, u32[]{:S(2)}) %collective-permute-start.2) | collective-permute-done | bytes 294944 | tf_op jit(solution)/shard_map/ppermute | solution.py:18
  97.4 2.6 %shard_map.89 = f32[256,1152]{1,0:T(8,128)} custom-call(f32[1]{0:T(128)S(6)} %copy.11.scale_ref, f32[1]{0:T(128)S(6)} %copy.12.shift_ref, bf16[272,1152]{1,0:T(8,128)(2,1)S(1)} %shard_map.86.packet_ref.refs_0_, bf16[128,1152]{1,0:T(8,128)(2,1)S(1)} %shard_map.88.refs_0_.block_ref, bf16[128,1152]{1,0:T(8,128)(2,1)S(1)} %collective-permute-done.refs_1_, ...), custom_call_target="tpu_custom_call" | custom-call | tf_op jit(solution)/shard_map/pallas_call | solution.py:209
  100.0 0.0 all-to-all-done.1.chunks_ref
  100.0 1.4 %shard_map.91 = f32[128,1152]{1,0:T(8,128)} custom-call(bf16[32,54,128]{2,1,0:T(8,128)(2,1)S(1)} %all-to-all-done.1.chunks_ref, s32[1,1,32,6]{3,2,1,0:T(8,128)S(1)} %copy.9.listed_ref, s32[1,32,32]{2,1,0:T(8,128)S(1)} %copy-done.2), custom_call_target="tpu_custom_call" | custom-call | tf_op jit(solution)/shard_map/pallas_call | solution.py:213
  (1 shorter events, 0.0 us)
Async XLA Ops:
  0.6 1.3 %copy-start = (f32[256,1152]{1,0:T(8,128)S(1)}, f32[256,1152]{1,0:T(8,128)}, u32[]{:S(2)}) copy-start(f32[256,1152]{1,0:T(8,128)} %refs_0_.1) | copy-start | bytes 3538948
  1.9 0.7 copy-start.3
  2.6 7.7 %copy-start.4 = (s32[1,1,32,6]{2,1,3,0:T(1,128)S(1)}, s32[1,1,32,6]{2,1,3,0:T(1,128)}, u32[]{:S(2)}) copy-start(s32[1,1,32,6]{2,1,3,0:T(1,128)} %param.9) | copy-start | bytes 2308
  2.6 7.8 %copy-start.1 = (f32[128,1152]{1,0:T(8,128)S(1)}, f32[128,1152]{1,0:T(8,128)}, u32[]{:S(2)}) copy-start(f32[128,1152]{1,0:T(8,128)} %caption_ref.1) | copy-start | bytes 1769476
  2.7 48.5 %copy-start.2 = (s32[1,32,32]{2,1,0:T(8,128)S(1)}, s32[1,32,32]{2,1,0:T(8,128)}, u32[]{:S(2)}) copy-start(s32[1,32,32]{2,1,0:T(8,128)} %tally_ref.5) | copy-start | bytes 12292
  2.7 32.0 %collective-permute-start.4 = (bf16[272,1152]{1,0:T(8,128)(2,1)S(1)}, bf16[272,1152]{1,0:T(8,128)(2,1)S(1)}, u32[]{:S(2)}, u32[]{:S(2)}) collective-permute-start(bf16[272,1152]{1,0:T(8,128)(2,1)S(1)} %shard_map.86.packet_ref.refs_0_), channel_id=1, source_target_pairs={{0,960},{32,992},{64,0},{96,32},{128,64},{160,96},{192,128},{224,1... | collective-permute-start | bytes 1880072 | tf_op jit(solution)/shard_map/ppermute | solution.py:18
  11.6 39.6 %all-to-all-start = ((bf16[32,54,128]{2,1,0:T(8,128)(2,1)}), bf16[32,54,128]{2,1,0:T(8,128)(2,1)S(1)}, u32[]{:S(2)}, u32[]{:S(2)}) async-start(bf16[32,54,128]{2,1,0:T(8,128)(2,1)} %shard_map.87), calls=%async_computation | async-start | bytes 917504 | tf_op jit(solution)/shard_map/all_to_all | solution.py:196
  32.7 19.1 %collective-permute-start.3 = (bf16[272,1152]{1,0:T(8,128)(2,1)S(1)}, bf16[272,1152]{1,0:T(8,128)(2,1)S(1)}, u32[]{:S(2)}, u32[]{:S(2)}) collective-permute-start(bf16[272,1152]{1,0:T(8,128)(2,1)S(1)} %shard_map.86.packet_ref.refs_0_), channel_id=1, source_target_pairs={{0,992},{32,0},{64,32},{96,64},{128,96},{160,128},{192,160},{224,1... | collective-permute-start | bytes 1880072 | tf_op jit(solution)/shard_map/ppermute | solution.py:18
  34.7 19.8 %collective-permute-start.5 = (bf16[272,1152]{1,0:T(8,128)(2,1)S(1)}, bf16[272,1152]{1,0:T(8,128)(2,1)S(1)}, u32[]{:S(2)}, u32[]{:S(2)}) collective-permute-start(bf16[272,1152]{1,0:T(8,128)(2,1)S(1)} %collective-permute-done.4.refs_2_), channel_id=1, source_target_pairs={{0,992},{32,0},{64,32},{96,64},{128,96},{160,128},{192,160},{224,1... | collective-permute-start | bytes 1880072 | tf_op jit(solution)/shard_map/ppermute | solution.py:18
  57.7 42.3 %all-to-all-start.1 = ((bf16[32,54,128]{2,1,0:T(8,128)(2,1)}), bf16[32,54,128]{2,1,0:T(8,128)(2,1)S(1)}, u32[]{:S(2)}, u32[]{:S(2)}) async-start(bf16[32,54,128]{2,1,0:T(8,128)(2,1)} %shard_map.90), calls=%async_computation.1 | async-start | bytes 917504 | tf_op jit(solution)/shard_map/all_to_all | solution.py:204
  70.3 16.9 %collective-permute-start.1 = (bf16[128,1152]{1,0:T(8,128)(2,1)S(1)}, bf16[128,1152]{1,0:T(8,128)(2,1)S(1)}, u32[]{:S(2)}, u32[]{:S(2)}) collective-permute-start(bf16[128,1152]{1,0:T(8,128)(2,1)S(1)} %shard_map.88.refs_0_.block_ref), channel_id=1, source_target_pairs={{0,64},{32,96},{64,128},{96,160},{128,192},{160,224},{192,256},{22... | collective-permute-start | bytes 884744 | tf_op jit(solution)/shard_map/ppermute | solution.py:18
  72.3 16.9 %collective-permute-start = (bf16[128,1152]{1,0:T(8,128)(2,1)S(1)}, bf16[128,1152]{1,0:T(8,128)(2,1)S(1)}, u32[]{:S(2)}, u32[]{:S(2)}) collective-permute-start(bf16[128,1152]{1,0:T(8,128)(2,1)S(1)} %shard_map.88.refs_0_.block_ref), channel_id=1, source_target_pairs={{0,32},{32,64},{64,96},{96,128},{128,160},{160,192},{192,224},{224... | collective-permute-start | bytes 884744 | tf_op jit(solution)/shard_map/ppermute | solution.py:18
  87.2 10.1 %collective-permute-start.2 = (bf16[128,1152]{1,0:T(8,128)(2,1)S(1)}, bf16[128,1152]{1,0:T(8,128)(2,1)S(1)}, u32[]{:S(2)}, u32[]{:S(2)}) collective-permute-start(bf16[128,1152]{1,0:T(8,128)(2,1)S(1)} %collective-permute-done.1.refs_2_), channel_id=1, source_target_pairs={{0,32},{32,64},{64,96},{96,128},{128,160},{160,192},{192,224},{224... | collective-permute-start | bytes 884744 | tf_op jit(solution)/shard_map/ppermute | solution.py:18

commit v2 on v1

--- a/solution.py
+++ b/solution.py
@@ -54,6 +54,14 @@
     ).astype(BF16)
 
 
+def upright(listed_ref):
+    peers = listed_ref.shape[2]
+    diagonal = iota((peers, peers), 0) == iota((peers, peers), 1)
+    return [
+        jnp.sum(jnp.where(diagonal, listed_ref[slot], 0), axis=1, keepdims=True) for slot in range(listed_ref.shape[0])
+    ]
+
+
 def block_places(tally, group_at, slot_cap, width):
     peers = tally.shape[0]
     mine = jnp.where(iota(tally.shape, 1) == group_at, tally, 0)
@@ -64,6 +72,12 @@
     return hits([jnp.where(incoming > slot, first + slot, -1) for slot in range(slot_cap)], width)
 
 
+def places_of(packet_ref, stop):
+    rows = packet_ref.shape[0] - AUX_ROWS
+    kept = packet_ref[rows:, 0:rows].astype(F32)
+    return jnp.sum(jnp.where(iota(kept.shape, 0) == stop, kept, 0.0), axis=0, keepdims=True).astype(jnp.int32)
+
+
 def slopes_for(text, image, places, scale, shift):
     scores = lax.dot_general(text, image, (((1,), (1,)), ((), ())), preferred_element_type=F32)
     logits = scale * scores + shift
@@ -72,22 +86,63 @@
     return (jnp.where(positive, -scale, scale) * toward).astype(BF16)
 
 
-def picture_kernel(loop_count, group_count, text_rows, picture_ref, positive_ref, packet_ref):
+def prepare_kernel(
+    loop_count,
+    group_count,
+    picture_hbm,
+    positive_hbm,
+    caption_hbm,
+    listed_hbm,
+    packet_ref,
+    chunks_ref,
+    picture_ref,
+    positive_ref,
+    caption_ref,
+    listed_ref,
+    staging,
+    arrived,
+):
+    copies = [
+        pltpu.make_async_copy(source, target, arrived.at[at])
+        for at, (source, target) in enumerate(
+            [
+                (listed_hbm, listed_ref),
+                (caption_hbm, caption_ref),
+                (positive_hbm, positive_ref),
+                (picture_hbm, picture_ref),
+            ]
+        )
+    ]
+    for copy in copies:
+        copy.start()
+    text_rows = caption_ref.shape[0]
+    copies[0].wait()
+    chosen = hits(upright(listed_ref), text_rows)
+    copies[1].wait()
+    gathered = jnp.dot(chosen, caption_ref[...].astype(BF16), preferred_element_type=F32)
+    rows_to_chunks(gathered, staging, chunks_ref)
     rows = picture_ref.shape[0]
-    packet_ref[0:rows, :] = picture_ref[...].astype(BF16)
+    copies[2].wait()
     positive = positive_ref[...]
     anchor = positive // (group_count * text_rows)
     behind = lax.rem(lax.axis_index("loop") - anchor + loop_count, loop_count)
     place = lax.rem(positive, text_rows)
     packet_ref[rows:, :] = jnp.zeros((AUX_ROWS, packet_ref.shape[1]), BF16)
     packet_ref[rows:, 0:rows] = jnp.where(behind == iota((AUX_ROWS, rows), 0), place, -1).astype(F32).astype(BF16)
-
-
-def dispatch_kernel(caption_ref, listed_ref, chunks_ref, staging):
-    listed = listed_ref[0, 0]
-    chosen = hits([listed[:, slot : slot + 1] for slot in range(listed.shape[1])], caption_ref.shape[0])
-    rows = jnp.dot(chosen, caption_ref[...].astype(BF16), preferred_element_type=F32)
-    rows_to_chunks(rows, staging, chunks_ref)
+    copies[3].wait()
+    packet_ref[0:rows, :] = picture_ref[...].astype(BF16)
+
+
+def relay_kernel(own_ref, arrived_ref, out_ref):
+    parity = lax.rem(lax.axis_index("loop"), 2)
+
+    @pl.when(parity == 1)
+    def _():
+        out_ref[...] = arrived_ref[...]
+
+    @pl.when(parity == 0)
+    def _():
+        out_ref[...] = own_ref[...]
 
 
 def assemble_kernel(chunks_ref, tally_ref, block_ref, staging, rows_ref):
@@ -100,15 +155,16 @@
 
 
 def text_kernel(scale_ref, shift_ref, tally_ref, block_ref, *refs):
-    packets, chunks_ref, staging = refs[:STOPS], refs[STOPS], refs[STOPS + 1]
+    packets, chunks_ref, staging = refs[:STOPS], *refs[STOPS:]
     scale, shift = scale_ref[0], shift_ref[0]
     text = block_ref[...]
     rows = packets[0].shape[0] - AUX_ROWS
+    odd = lax.rem(lax.axis_index("loop"), 2)
     total = jnp.zeros(text.shape, F32)
-    for stop, packet in enumerate(packets):
+    for stop, packet in zip((0, 2, 1 + 2 * odd, 3 - 2 * odd), packets):
         image = packet[0:rows, :]
-        places = packet[rows:, 0:rows].astype(F32)[stop : stop + 1, :].astype(jnp.int32)
-        total = total + jnp.dot(slopes_for(text, image, places, scale, shift), image, preferred_element_type=F32)
+        slopes = slopes_for(text, image, places_of(packet, stop), scale, shift)
+        total = total + jnp.dot(slopes, image, preferred_element_type=F32)
     slot_cap = chunks_ref.shape[1] * LANES // text.shape[1]
     slots = block_places(tally_ref[0], lax.axis_index("grp"), slot_cap, text.shape[0])
     rows_to_chunks(jnp.dot(slots, total.astype(BF16), preferred_element_type=F32), staging, chunks_ref)
@@ -119,10 +175,10 @@
     scale, shift = scale_ref[0], shift_ref[0]
     rows = grad_ref.shape[0]
     image = packet_ref[0:rows, :]
-    aux = packet_ref[rows:, 0:rows].astype(F32)
+    odd = lax.rem(lax.axis_index("loop"), 2)
     slopes = [
-        slopes_for(block[...], image, aux[stop : stop + 1, :].astype(jnp.int32), scale, shift)
-        for stop, block in enumerate(blocks)
+        slopes_for(block[...], image, places_of(packet_ref, stop), scale, shift)
+        for stop, block in zip((0, 2, 3 - 2 * odd, 1 + 2 * odd), blocks)
     ]
     width = 3 * LANES
     for start in range(0, grad_ref.shape[1], width):
@@ -137,13 +193,13 @@
 
 def return_kernel(chunks_ref, listed_ref, tally_ref, grad_ref, staging, rows_ref):
     chunks_to_rows(chunks_ref, staging, rows_ref)
-    listed, tally = listed_ref[0, 0], tally_ref[0]
-    peers, slot_cap = listed.shape
+    tally = tally_ref[0]
+    peers = tally.shape[0]
     mine = jnp.sum(jnp.where(iota(tally.shape, 0) == lax.axis_index("grp"), tally, 0), axis=0, keepdims=True)
-    upright = iota((peers, peers), 0) == iota((peers, peers), 1)
-    outgoing = jnp.sum(jnp.where(upright, mine, 0), axis=1, keepdims=True)
+    diagonal = iota((peers, peers), 0) == iota((peers, peers), 1)
+    outgoing = jnp.sum(jnp.where(diagonal, mine, 0), axis=1, keepdims=True)
     owned = hits(
-        [jnp.where(outgoing > slot, listed[:, slot : slot + 1], -1) for slot in range(slot_cap)], grad_ref.shape[0]
+        [jnp.where(outgoing > slot, rows, -1) for slot, rows in enumerate(upright(listed_ref))], grad_ref.shape[0]
     )
     grad_ref[...] = lax.dot_general(owned, rows_ref[...], (((0,), (0,)), ((), ())), preferred_element_type=F32)
 
@@ -167,52 +223,99 @@
 
     whole = pl.BlockSpec(memory_space=pltpu.VMEM)
     scalar = pl.BlockSpec(memory_space=pltpu.SMEM)
-    params = pltpu.CompilerParams(vmem_limit_bytes=48 * 1024 * 1024)
+    remote = pl.BlockSpec(memory_space=pltpu.HBM)
     staging = pltpu.VMEM((group_count * pitch, LANES), F32)
     slot_rows = pltpu.VMEM((group_count * slot_cap, features), BF16)
     chunks = jax.ShapeDtypeStruct((group_count, chunk_rows, LANES), BF16)
-
-    def call(kernel, in_specs, out_shape, scratch=()):
+    packet_shape = jax.ShapeDtypeStruct((image_rows + AUX_ROWS, features), BF16)
+    big = pl.CostEstimate(flops=6 * STOPS * image_rows * text_rows * features, bytes_accessed=8 * image_rows * features, transcendentals=0)
+    huge = pl.CostEstimate(flops=50 * 1000 * 1000 * 1000, bytes_accessed=0, transcendentals=0)
+    block_shape = jax.ShapeDtypeStruct((text_rows, features), BF16)
+
+    def in_vmem(shape):
+        return pltpu.VMEM(shape.shape, shape.dtype)
+
+    def call(kernel, in_specs, out_shape, scratch=(), name=None, cost=None, limit=24):
         return pl.pallas_call(
             kernel,
             out_shape=out_shape,
             in_specs=in_specs,
-            out_specs=whole,
+            out_specs=jax.tree.map(lambda _: whole, out_shape),
             scratch_shapes=list(scratch),
-            compiler_params=params,
+            compiler_params=pltpu.CompilerParams(vmem_limit_bytes=limit * 1024 * 1024),
+            name=name,
+            cost_estimate=cost,
         )
 
-    def picture_body(*refs):
-        picture_kernel(loop_count, group_count, text_rows, *refs)
-
-    packet = call(
-        picture_body, [whole] * 2, jax.ShapeDtypeStruct((image_rows + AUX_ROWS, features), BF16)
-    )(picture_features, positive_caption_position.reshape(1, -1))
+    def prepare_body(*refs):
+        prepare_kernel(loop_count, group_count, *refs)
+
+    def swapped(value):
+        return lax.ppermute(value, "loop", [(source, source ^ 1) for source in range(loop_count)])
+
+    listed = jnp.transpose(dispatched_entries[0], (2, 0, 1))
+    packet, outgoing = call(
+        prepare_body,
+        [remote] * 4,
+        (in_vmem(packet_shape), in_vmem(chunks)),
+        [
+            pltpu.VMEM(picture_features.shape, F32),
+            pltpu.VMEM((1, image_rows), jnp.int32),
+            pltpu.VMEM(caption_features_per_holder.shape, F32),
+            pltpu.VMEM(listed.shape, jnp.int32),
+            staging,
+            pltpu.SemaphoreType.DMA((4,)),
+        ],
+        name="prepare",
+    )(
+        *[
+            pltpu.with_memory_space_constraint(each, pltpu.HBM)
+            for each in (
+                picture_features,
+                positive_caption_position.reshape(1, -1),
+                caption_features_per_holder,
+                listed,
+            )
+        ]
+    )
+
     packet_two = passed_along(packet, "loop", -2)
-    packet_one = passed_along(packet, "loop", -1)
-    packet_three = passed_along(packet_two, "loop", -1)
-
-    outgoing = call(dispatch_kernel, [whole] * 2, chunks, [staging])(caption_features_per_holder, dispatched_entries)
+    packet_relay = lax.ppermute(
+        packet, "loop", [(source, (source - 3 + 2 * (source % 2)) % loop_count) for source in range(loop_count)]
+    )
     incoming = lax.all_to_all(outgoing, "grp", split_axis=0, concat_axis=0, tiled=True)
-    block = call(
-        assemble_kernel, [whole] * 2, jax.ShapeDtypeStruct((text_rows, features), BF16), [staging, slot_rows]
-    )(incoming, sent_tally)
-
-    sendback = call(text_kernel, [scalar] * 2 + [whole] * (2 + STOPS), chunks, [staging])(
-        score_scale_factor, score_shift_term, sent_tally, block, packet, packet_one, packet_two, packet_three
-    )
+    packet_swap = swapped(packet_two)
+
+    block = call(assemble_kernel, [whole] * 2, in_vmem(block_shape), [staging, slot_rows], name="assemble")(
+        incoming, sent_tally
+    )
+    block_two = passed_along(block, "loop", 2)
+
+    sendback = call(
+        text_kernel, [scalar] * 2 + [whole] * (2 + STOPS), in_vmem(chunks), [staging], name="text_grads", cost=big
+    )(score_scale_factor, score_shift_term, sent_tally, block, packet, packet_two, packet_relay, packet_swap)
     returned = lax.all_to_all(sendback, "grp", split_axis=0, concat_axis=0, tiled=True)
 
-    block_two = passed_along(block, "loop", 2)
-    block_one = passed_along(block, "loop", 1)
-    block_three = passed_along(block_two, "loop", 1)
+    relayed_block = call(relay_kernel, [whole] * 2, in_vmem(block_shape), name="relay_blocks", cost=huge)(
+        block, block_two
+    )
+    block_relay = passed_along(relayed_block, "loop", 1)
+    block_swap = swapped(block_two)
     image_grad = call(
-        image_kernel, [scalar] * 2 + [whole] * (1 + STOPS), jax.ShapeDtypeStruct((image_rows, features), F32)
-    )(score_scale_factor, score_shift_term, packet, block, block_one, block_two, block_three)
+        image_kernel,
+        [scalar] * 2 + [whole] * (1 + STOPS),
+        jax.ShapeDtypeStruct((image_rows, features), F32),
+        name="image_grads",
+        cost=big,
+    )(score_scale_factor, score_shift_term, packet, block, block_two, block_relay, block_swap)
 
     text_grad = call(
-        return_kernel, [whole] * 3, jax.ShapeDtypeStruct((text_rows, features), F32), [staging, slot_rows]
-    )(returned, dispatched_entries, sent_tally)
+        return_kernel,
+        [whole] * 3,
+        jax.ShapeDtypeStruct((text_rows, features), F32),
+        [staging, slot_rows],
+        name="give_back",
+    )(returned, listed, sent_tally)
     return (image_grad, text_grad)
 
 

time: 102 us -> 91.4 us (0.90)
  the two profiles are of different devices: /device:TPU:16 before, /device:TPU:28 now
where the time goes in v2:
time: 91.4 us; the launch traced here: 90.8 us
  starting transfers between devices  51.2 us (56%)
  waiting for transfers between devices  25.7 us (28%)
  Pallas kernels  11.9 us (13%)
  between operations  2.06 us (2%)
    all_to_all x1, starting transfers between devices, local(): lax.all_to_all(outgoing, 'grp', split_axis=0, concat_axis=0, tiled=True)  22 us
    all_to_all x1, waiting for transfers between devices, local(): lax.all_to_all(outgoing, 'grp', split_axis=0, concat_axis=0, tiled=True)  15 us
    ppermute x3, starting transfers between devices, passed_along(): return lax.ppermute(value, axis, pairs)  14.1 us
    all_to_all x1, starting transfers between devices, local(): lax.all_to_all(sendback, 'grp', split_axis=0, concat_axis=0, tiled=True)  8.78 us
    all_to_all x1, waiting for transfers between devices, local(): lax.all_to_all(sendback, 'grp', split_axis=0, concat_axis=0, tiled=True)  6.54 us
    ppermute x2, starting transfers between devices, swapped(): lax.ppermute(value, 'loop', [(source, source ^ 1) for source in range(loo...  4.42 us
    ppermute x3, waiting for transfers between devices, passed_along(): return lax.ppermute(value, axis, pairs)  4.1 us
    pallas_call x1, Pallas kernels, local(): call(image_kernel, [scalar] * 2 + [whole] * (1 + STOPS), jax.ShapeDtypeSt...  3.56 us
  transfers between devices with their start and end apart: 8, of which 3 were waited for; matrix products, arithmetic and copies ran while one was open for 0% of the time, Pallas kernels for 9%

profile of v2, /device:TPU:28, one launch (start us, length us, event | category | flops | bytes accessed | tf_op | source)
XLA Modules:
  0.0 90.8 jit_solution(11931050830933039880)
XLA Ops:
  0.6 0.0 copy-start
  0.6 2.3 %prepare.1 = (bf16[272,1152]{1,0:T(8,128)(2,1)S(1)}, bf16[32,54,128]{2,1,0:T(8,128)(2,1)}) custom-call(f32[256,1152]{1,0:T(8,128)} %refs_0_.1, s32[1,256]{1,0:T(1,128)} %bitcast.6, f32[128,1152]{1,0:T(8,128)} %refs_2_.1, s32[6,1,32]{2,1,0:T(1,128)} %bitcast.4), custom_call_target="tpu_custom_call" | custom-call | tf_op jit(solution)/shard_map/prepare/pallas_call | solution.py:257
  2.9 3.3 %collective-permute-start.3 = (bf16[272,1152]{1,0:T(8,128)(2,1)S(1)}, bf16[272,1152]{1,0:T(8,128)(2,1)S(1)}, u32[]{:S(2)}, u32[]{:S(2)}) collective-permute-start(bf16[272,1152]{1,0:T(8,128)(2,1)S(1)} %get-tuple-element.4.packet_ref.refs_0_), channel_id=1, source_target_pairs={{0,960},{32,992},{64,0},{96,32},{128,64},{160,96},{192,128},{224,1... | collective-permute-start | bytes 1880072 | tf_op jit(solution)/shard_map/ppermute | solution.py:18
  6.3 22.0 %all-to-all-start = ((bf16[32,54,128]{2,1,0:T(8,128)(2,1)}), bf16[32,54,128]{2,1,0:T(8,128)(2,1)S(1)}, u32[]{:S(2)}, u32[]{:S(2)}) async-start(bf16[32,54,128]{2,1,0:T(8,128)(2,1)} %get-tuple-element.5), calls=%async_computation | async-start | bytes 917504 | tf_op jit(solution)/shard_map/all_to_all | solution.py:286
  28.3 1.9 %collective-permute-start.4 = (bf16[272,1152]{1,0:T(8,128)(2,1)S(1)}, bf16[272,1152]{1,0:T(8,128)(2,1)S(1)}, u32[]{:S(2)}, u32[]{:S(2)}) collective-permute-start(bf16[272,1152]{1,0:T(8,128)(2,1)S(1)} %get-tuple-element.4.packet_ref.refs_0_), channel_id=1, source_target_pairs={{0,928},{32,0},{64,992},{96,64},{128,32},{160,128},{192,96},{224,1... | collective-permute-start | bytes 1880072 | tf_op jit(solution)/shard_map/ppermute | solution.py:283
  30.2 0.0 collective-permute-done.3.refs_1_
  30.2 2.4 %collective-permute-start.5 = (bf16[272,1152]{1,0:T(8,128)(2,1)S(1)}, bf16[272,1152]{1,0:T(8,128)(2,1)S(1)}, u32[]{:S(2)}, u32[]{:S(2)}) collective-permute-start(bf16[272,1152]{1,0:T(8,128)(2,1)S(1)} %collective-permute-done.3.refs_1_), channel_id=1, source_target_pairs={{0,32},{32,0},{64,96},{96,64},{128,160},{160,128},{192,224},{224,1... | collective-permute-start | bytes 1880072 | tf_op jit(solution)/shard_map/ppermute | solution.py:254
  32.6 15.0 %all-to-all-done.chunks_ref = bf16[32,54,128]{2,1,0:T(8,128)(2,1)S(1)} async-done(((bf16[32,54,128]{2,1,0:T(8,128)(2,1)}), bf16[32,54,128]{2,1,0:T(8,128)(2,1)S(1)}, u32[]{:S(2)}, u32[]{:S(2)}) %all-to-all-start) | async-done | bytes 442400 | tf_op jit(solution)/shard_map/all_to_all | solution.py:286
  47.7 0.0 copy-done
  47.7 0.6 assemble.1.own_ref.refs_0_.block_ref
  48.3 8.8 %collective-permute-start = (bf16[128,1152]{1,0:T(8,128)(2,1)S(1)}, bf16[128,1152]{1,0:T(8,128)(2,1)}, u32[]{:S(2)}, u32[]{:S(2)}) collective-permute-start(bf16[128,1152]{1,0:T(8,128)(2,1)S(1)} %assemble.1.own_ref.refs_0_.block_ref), channel_id=1, source_target_pairs={{0,64},{32,96},{64,128},{96,160},{128,192},{160,224},{192,256},{22... | collective-permute-start | bytes 884744 | tf_op jit(solution)/shard_map/ppermute | solution.py:18
  58.4 0.0 collective-permute-done.4.refs_2_
  58.4 0.0 collective-permute-done.5.refs_3_
  58.4 3.2 %text_grads.1 = bf16[32,54,128]{2,1,0:T(8,128)(2,1)} custom-call(f32[1]{0:T(128)S(6)} %copy.9.scale_ref, f32[1]{0:T(128)S(6)} %copy.10.shift_ref, s32[1,32,32]{2,1,0:T(8,128)S(1)} %copy-done, bf16[128,1152]{1,0:T(8,128)(2,1)S(1)} %assemble.1.own_ref.refs_0_.block_ref, bf16[272,1152]{1,0:T(8,128)(2,1)S(1)} %get-tuple-element.4.packet_ref.refs_0_, ...), custom_call_target="tpu_custom_call" | custom-call | flops 905969664 | bytes 2359296 | tf_op jit(solution)/shard_map/text_grads/pallas_call | solution.py:294
  61.6 8.8 %all-to-all-start.1 = ((bf16[32,54,128]{2,1,0:T(8,128)(2,1)}), bf16[32,54,128]{2,1,0:T(8,128)(2,1)S(1)}, u32[]{:S(2)}, u32[]{:S(2)}) async-start(bf16[32,54,128]{2,1,0:T(8,128)(2,1)} %text_grads.1), calls=%async_computation.1 | async-start | bytes 917504 | tf_op jit(solution)/shard_map/all_to_all | solution.py:297
  70.3 0.0 collective-permute-done.arrived_ref.refs_1_
  70.4 1.0 %relay_blocks.1 = bf16[128,1152]{1,0:T(8,128)(2,1)S(1)} custom-call(bf16[128,1152]{1,0:T(8,128)(2,1)S(1)} %assemble.1.own_ref.refs_0_.block_ref, bf16[128,1152]{1,0:T(8,128)(2,1)} %collective-permute-done.arrived_ref.refs_1_), custom_call_target="tpu_custom_call" | custom-call | flops 49999998976 | tf_op jit(solution)/shard_map/relay_blocks/pallas_call | solution.py:299
  71.3 0.0 copy-start.1
  71.4 1.9 %collective-permute-start.1 = (bf16[128,1152]{1,0:T(8,128)(2,1)S(1)}, bf16[128,1152]{1,0:T(8,128)(2,1)S(1)}, u32[]{:S(2)}, u32[]{:S(2)}) collective-permute-start(bf16[128,1152]{1,0:T(8,128)(2,1)S(1)} %relay_blocks.1), channel_id=1, source_target_pairs={{0,32},{32,64},{64,96},{96,128},{128,160},{160,192},{192,224},{224... | collective-permute-start | bytes 884744 | tf_op jit(solution)/shard_map/ppermute | solution.py:18
  73.3 2.0 %collective-permute-start.2 = (bf16[128,1152]{1,0:T(8,128)(2,1)}, bf16[128,1152]{1,0:T(8,128)(2,1)S(1)}, u32[]{:S(2)}, u32[]{:S(2)}) collective-permute-start(bf16[128,1152]{1,0:T(8,128)(2,1)} %collective-permute-done.arrived_ref.refs_1_), channel_id=1, source_target_pairs={{0,32},{32,0},{64,96},{96,64},{128,160},{160,128},{192,224},{224,1... | collective-permute-start | bytes 884744 | tf_op jit(solution)/shard_map/ppermute | solution.py:254
  75.3 4.1 %collective-permute-done.1.refs_2_ = bf16[128,1152]{1,0:T(8,128)(2,1)S(1)} collective-permute-done((bf16[128,1152]{1,0:T(8,128)(2,1)S(1)}, bf16[128,1152]{1,0:T(8,128)(2,1)S(1)}, u32[]{:S(2)}, u32[]{:S(2)}) %collective-permute-start.1) | collective-permute-done | bytes 294944 | tf_op jit(solution)/shard_map/ppermute | solution.py:18
  79.4 0.0 collective-permute-done.2.refs_3_
  79.4 3.6 %image_grads.1 = f32[256,1152]{1,0:T(8,128)} custom-call(f32[1]{0:T(128)S(6)} %copy.9.scale_ref, f32[1]{0:T(128)S(6)} %copy.10.shift_ref, bf16[272,1152]{1,0:T(8,128)(2,1)S(1)} %get-tuple-element.4.packet_ref.refs_0_, bf16[128,1152]{1,0:T(8,128)(2,1)S(1)} %assemble.1.own_ref.refs_0_.block_ref, bf16[128,1152]{1,0:T(8,128)(2,1)} %collective-permute-done.arrived_ref.refs_1_, ...), custom_call_target="tpu_custom_call" | custom-call | flops 905969664 | bytes 2359296 | tf_op jit(solution)/shard_map/image_grads/pallas_call | solution.py:304
  83.0 6.5 %all-to-all-done.1.chunks_ref = bf16[32,54,128]{2,1,0:T(8,128)(2,1)S(1)} async-done(((bf16[32,54,128]{2,1,0:T(8,128)(2,1)}), bf16[32,54,128]{2,1,0:T(8,128)(2,1)S(1)}, u32[]{:S(2)}, u32[]{:S(2)}) %all-to-all-start.1) | async-done | bytes 442400 | tf_op jit(solution)/shard_map/all_to_all | solution.py:297
  89.5 0.0 copy-done.1
  89.5 1.3 %give_back.1 = f32[128,1152]{1,0:T(8,128)} custom-call(bf16[32,54,128]{2,1,0:T(8,128)(2,1)S(1)} %all-to-all-done.1.chunks_ref, s32[6,1,32]{2,1,0:T(1,128)S(1)} %bitcast.5, s32[1,32,32]{2,1,0:T(8,128)S(1)} %copy-done), custom_call_target="tpu_custom_call" | custom-call | tf_op jit(solution)/shard_map/give_back/pallas_call | solution.py:312
Async XLA Ops:
  0.6 47.0 %copy-start = (s32[1,32,32]{2,1,0:T(8,128)S(1)}, s32[1,32,32]{2,1,0:T(8,128)}, u32[]{:S(2)}) copy-start(s32[1,32,32]{2,1,0:T(8,128)} %tally_ref.5) | copy-start | bytes 12292
  2.9 27.3 %collective-permute-start.3 = (bf16[272,1152]{1,0:T(8,128)(2,1)S(1)}, bf16[272,1152]{1,0:T(8,128)(2,1)S(1)}, u32[]{:S(2)}, u32[]{:S(2)}) collective-permute-start(bf16[272,1152]{1,0:T(8,128)(2,1)S(1)} %get-tuple-element.4.packet_ref.refs_0_), channel_id=1, source_target_pairs={{0,960},{32,992},{64,0},{96,32},{128,64},{160,96},{192,128},{224,1... | collective-permute-start | bytes 1880072 | tf_op jit(solution)/shard_map/ppermute | solution.py:18
  6.3 41.4 %all-to-all-start = ((bf16[32,54,128]{2,1,0:T(8,128)(2,1)}), bf16[32,54,128]{2,1,0:T(8,128)(2,1)S(1)}, u32[]{:S(2)}, u32[]{:S(2)}) async-start(bf16[32,54,128]{2,1,0:T(8,128)(2,1)} %get-tuple-element.5), calls=%async_computation | async-start | bytes 917504 | tf_op jit(solution)/shard_map/all_to_all | solution.py:286
  28.3 30.1 %collective-permute-start.4 = (bf16[272,1152]{1,0:T(8,128)(2,1)S(1)}, bf16[272,1152]{1,0:T(8,128)(2,1)S(1)}, u32[]{:S(2)}, u32[]{:S(2)}) collective-permute-start(bf16[272,1152]{1,0:T(8,128)(2,1)S(1)} %get-tuple-element.4.packet_ref.refs_0_), channel_id=1, source_target_pairs={{0,928},{32,0},{64,992},{96,64},{128,32},{160,128},{192,96},{224,1... | collective-permute-start | bytes 1880072 | tf_op jit(solution)/shard_map/ppermute | solution.py:283
  30.2 28.2 %collective-permute-start.5 = (bf16[272,1152]{1,0:T(8,128)(2,1)S(1)}, bf16[272,1152]{1,0:T(8,128)(2,1)S(1)}, u32[]{:S(2)}, u32[]{:S(2)}) collective-permute-start(bf16[272,1152]{1,0:T(8,128)(2,1)S(1)} %collective-permute-done.3.refs_1_), channel_id=1, source_target_pairs={{0,32},{32,0},{64,96},{96,64},{128,160},{160,128},{192,224},{224,1... | collective-permute-start | bytes 1880072 | tf_op jit(solution)/shard_map/ppermute | solution.py:254
  48.3 22.1 %collective-permute-start = (bf16[128,1152]{1,0:T(8,128)(2,1)S(1)}, bf16[128,1152]{1,0:T(8,128)(2,1)}, u32[]{:S(2)}, u32[]{:S(2)}) collective-permute-start(bf16[128,1152]{1,0:T(8,128)(2,1)S(1)} %assemble.1.own_ref.refs_0_.block_ref), channel_id=1, source_target_pairs={{0,64},{32,96},{64,128},{96,160},{128,192},{160,224},{192,256},{22... | collective-permute-start | bytes 884744 | tf_op jit(solution)/shard_map/ppermute | solution.py:18
  61.6 27.9 %all-to-all-start.1 = ((bf16[32,54,128]{2,1,0:T(8,128)(2,1)}), bf16[32,54,128]{2,1,0:T(8,128)(2,1)S(1)}, u32[]{:S(2)}, u32[]{:S(2)}) async-start(bf16[32,54,128]{2,1,0:T(8,128)(2,1)} %text_grads.1), calls=%async_computation.1 | async-start | bytes 917504 | tf_op jit(solution)/shard_map/all_to_all | solution.py:297
  71.3 18.2 %copy-start.1 = (s32[1,1,32,6]{2,1,3,0:T(1,128)S(1)}, s32[1,1,32,6]{2,1,3,0:T(1,128)}, u32[]{:S(2)}) copy-start(s32[1,1,32,6]{2,1,3,0:T(1,128)} %param.9) | copy-start | bytes 2308
  71.4 8.0 %collective-permute-start.1 = (bf16[128,1152]{1,0:T(8,128)(2,1)S(1)}, bf16[128,1152]{1,0:T(8,128)(2,1)S(1)}, u32[]{:S(2)}, u32[]{:S(2)}) collective-permute-start(bf16[128,1152]{1,0:T(8,128)(2,1)S(1)} %relay_blocks.1), channel_id=1, source_target_pairs={{0,32},{32,64},{64,96},{96,128},{128,160},{160,192},{192,224},{224... | collective-permute-start | bytes 884744 | tf_op jit(solution)/shard_map/ppermute | solution.py:18
  73.3 6.1 %collective-permute-start.2 = (bf16[128,1152]{1,0:T(8,128)(2,1)}, bf16[128,1152]{1,0:T(8,128)(2,1)S(1)}, u32[]{:S(2)}, u32[]{:S(2)}) collective-permute-start(bf16[128,1152]{1,0:T(8,128)(2,1)} %collective-permute-done.arrived_ref.refs_1_), channel_id=1, source_target_pairs={{0,32},{32,0},{64,96},{96,64},{128,160},{160,128},{192,224},{224,1... | collective-permute-start | bytes 884744 | tf_op jit(solution)/shard_map/ppermute | solution.py:254

commit v3 on v2

--- a/solution.py
+++ b/solution.py
@@ -8,6 +8,8 @@
 STOPS = 4
 LANES = 128
 AUX_ROWS = 16
+PARTS = 4
+WIDTH = 3 * LANES
 BF16 = jnp.bfloat16
 F32 = jnp.float32
 
@@ -22,7 +24,7 @@
     return lax.broadcasted_iota(jnp.int32, shape, dim)
 
 
-def rows_to_chunks(rows, staging, chunks_ref):
+def rows_to_chunks(rows, staging, chunks_ref, chunks_hbm, sent):
     peers, chunk_rows, _ = chunks_ref.shape
     pitch = staging.shape[0] // peers
     tiles = rows.shape[1] // LANES
@@ -31,8 +33,15 @@
             staging[pl.ds(slot * tiles + tile, peers, stride=pitch), :] = rows[
                 slot * peers : (slot + 1) * peers, tile * LANES : (tile + 1) * LANES
             ]
-    for peer in range(peers):
-        chunks_ref[peer] = staging[peer * pitch : peer * pitch + chunk_rows, :].astype(chunks_ref.dtype)
+    group = peers // PARTS
+    copies = []
+    for part in range(PARTS):
+        for peer in range(part * group, (part + 1) * group):
+            chunks_ref[peer] = staging[peer * pitch : peer * pitch + chunk_rows, :].astype(chunks_ref.dtype)
+        at = pl.ds(part * group, group)
+        copies.append(pltpu.make_async_copy(chunks_ref.at[at], chunks_hbm.at[at], sent.at[part]))
+        copies[-1].start()
+    return copies
 
 
 def chunks_to_rows(chunks_ref, staging, rows_ref):
@@ -94,13 +103,15 @@
     caption_hbm,
     listed_hbm,
     packet_ref,
-    chunks_ref,
+    chunks_hbm,
     picture_ref,
     positive_ref,
     caption_ref,
     listed_ref,
     staging,
+    chunks_ref,
     arrived,
+    sent,
 ):
     copies = [
         pltpu.make_async_copy(source, target, arrived.at[at])
@@ -120,7 +131,7 @@
     chosen = hits(upright(listed_ref), text_rows)
     copies[1].wait()
     gathered = jnp.dot(chosen, caption_ref[...].astype(BF16), preferred_element_type=F32)
-    rows_to_chunks(gathered, staging, chunks_ref)
+    leaving = rows_to_chunks(gathered, staging, chunks_ref, chunks_hbm, sent)
     rows = picture_ref.shape[0]
     copies[2].wait()
     positive = positive_ref[...]
@@ -131,6 +142,8 @@
     packet_ref[rows:, 0:rows] = jnp.where(behind == iota((AUX_ROWS, rows), 0), place, -1).astype(F32).astype(BF16)
     copies[3].wait()
     packet_ref[0:rows, :] = picture_ref[...].astype(BF16)
+    for copy in leaving:
+        copy.wait()
 
 
 def relay_kernel(own_ref, arrived_ref, out_ref):
@@ -154,8 +167,8 @@
     ).astype(BF16)
 
 
-def text_kernel(scale_ref, shift_ref, tally_ref, block_ref, *refs):
-    packets, chunks_ref, staging = refs[:STOPS], *refs[STOPS:]
+def text_kernel(scale_ref, shift_ref, block_ref, *refs):
+    packets, grad_ref = refs[:STOPS], refs[STOPS]
     scale, shift = scale_ref[0], shift_ref[0]
     text = block_ref[...]
     rows = packets[0].shape[0] - AUX_ROWS
@@ -165,13 +178,29 @@
         image = packet[0:rows, :]
         slopes = slopes_for(text, image, places_of(packet, stop), scale, shift)
         total = total + jnp.dot(slopes, image, preferred_element_type=F32)
-    slot_cap = chunks_ref.shape[1] * LANES // text.shape[1]
-    slots = block_places(tally_ref[0], lax.axis_index("grp"), slot_cap, text.shape[0])
-    rows_to_chunks(jnp.dot(slots, total.astype(BF16), preferred_element_type=F32), staging, chunks_ref)
+    grad_ref[...] = total.astype(BF16)
+
+
+def send_kernel(tally_ref, grad_ref, chunks_hbm, staging, chunks_ref, sent):
+    rows, width = grad_ref.shape
+    slot_cap = chunks_ref.shape[1] * LANES // width
+    slots = block_places(tally_ref[0], lax.axis_index("grp"), slot_cap, rows)
+    gathered = jnp.dot(slots, grad_ref[...], preferred_element_type=F32)
+    for copy in rows_to_chunks(gathered, staging, chunks_ref, chunks_hbm, sent):
+        copy.wait()
+
+
+def column_copies(source_ref, target_hbm, sent):
+    return [
+        pltpu.make_async_copy(
+            source_ref.at[:, pl.ds(start, WIDTH)], target_hbm.at[:, pl.ds(start, WIDTH)], sent.at[start // WIDTH]
+        )
+        for start in range(0, source_ref.shape[1], WIDTH)
+    ]
 
 
 def image_kernel(scale_ref, shift_ref, packet_ref, *refs):
-    blocks, grad_ref = refs[:STOPS], refs[STOPS]
+    blocks, grad_hbm, grad_ref, sent = refs[:STOPS], *refs[STOPS:]
     scale, shift = scale_ref[0], shift_ref[0]
     rows = grad_ref.shape[0]
     image = packet_ref[0:rows, :]
@@ -180,18 +209,20 @@
         slopes_for(block[...], image, places_of(packet_ref, stop), scale, shift)
         for stop, block in zip((0, 2, 3 - 2 * odd, 1 + 2 * odd), blocks)
     ]
-    width = 3 * LANES
-    for start in range(0, grad_ref.shape[1], width):
+    copies = column_copies(grad_ref, grad_hbm, sent)
+    for part, copy in enumerate(copies):
+        columns = slice(part * WIDTH, (part + 1) * WIDTH)
         total = None
         for slope, block in zip(slopes, blocks):
-            part = lax.dot_general(
-                slope, block[:, start : start + width], (((0,), (0,)), ((), ())), preferred_element_type=F32
-            )
-            total = part if total is None else total + part
-        grad_ref[:, start : start + width] = total
-
-
-def return_kernel(chunks_ref, listed_ref, tally_ref, grad_ref, staging, rows_ref):
+            term = lax.dot_general(slope, block[:, columns], (((0,), (0,)), ((), ())), preferred_element_type=F32)
+            total = term if total is None else total + term
+        grad_ref[:, columns] = total
+        copy.start()
+    for copy in copies:
+        copy.wait()
+
+
+def return_kernel(chunks_ref, listed_ref, tally_ref, grad_hbm, staging, rows_ref, grad_ref, sent):
     chunks_to_rows(chunks_ref, staging, rows_ref)
     tally = tally_ref[0]
     peers = tally.shape[0]
@@ -201,7 +232,15 @@
     owned = hits(
         [jnp.where(outgoing > slot, rows, -1) for slot, rows in enumerate(upright(listed_ref))], grad_ref.shape[0]
     )
-    grad_ref[...] = lax.dot_general(owned, rows_ref[...], (((0,), (0,)), ((), ())), preferred_element_type=F32)
+    copies = column_copies(grad_ref, grad_hbm, sent)
+    for part, copy in enumerate(copies):
+        columns = slice(part * WIDTH, (part + 1) * WIDTH)
+        grad_ref[:, columns] = lax.dot_general(
+            owned, rows_ref[:, columns], (((0,), (0,)), ((), ())), preferred_element_type=F32
+        )
+        copy.start()
+    for copy in copies:
+        copy.wait()
 
 
 def local(
@@ -232,17 +271,20 @@
     huge = pl.CostEstimate(flops=50 * 1000 * 1000 * 1000, bytes_accessed=0, transcendentals=0)
     block_shape = jax.ShapeDtypeStruct((text_rows, features), BF16)
 
+    leaving = pltpu.VMEM(chunks.shape, BF16)
+    column_sems = pltpu.SemaphoreType.DMA((features // WIDTH,))
+
     def in_vmem(shape):
         return pltpu.VMEM(shape.shape, shape.dtype)
 
-    def call(kernel, in_specs, out_shape, scratch=(), name=None, cost=None, limit=24):
+    def call(kernel, in_specs, out_shape, scratch=(), name=None, cost=None, outs=None):
         return pl.pallas_call(
             kernel,
             out_shape=out_shape,
             in_specs=in_specs,
-            out_specs=jax.tree.map(lambda _: whole, out_shape),
+            out_specs=jax.tree.map(lambda _: whole, out_shape) if outs is None else outs,
             scratch_shapes=list(scratch),
-            compiler_params=pltpu.CompilerParams(vmem_limit_bytes=limit * 1024 * 1024),
+            compiler_params=pltpu.CompilerParams(vmem_limit_bytes=24 * 1024 * 1024),
             name=name,
             cost_estimate=cost,
         )
@@ -257,16 +299,19 @@
     packet, outgoing = call(
         prepare_body,
         [remote] * 4,
-        (in_vmem(packet_shape), in_vmem(chunks)),
+        (in_vmem(packet_shape), chunks),
         [
             pltpu.VMEM(picture_features.shape, F32),
             pltpu.VMEM((1, image_rows), jnp.int32),
             pltpu.VMEM(caption_features_per_holder.shape, F32),
             pltpu.VMEM(listed.shape, jnp.int32),
             staging,
+            leaving,
             pltpu.SemaphoreType.DMA((4,)),
+            pltpu.SemaphoreType.DMA((PARTS,)),
         ],
         name="prepare",
+        outs=(whole, remote),
     )(
         *[
             pltpu.with_memory_space_constraint(each, pltpu.HBM)
@@ -289,11 +334,20 @@
     block = call(assemble_kernel, [whole] * 2, in_vmem(block_shape), [staging, slot_rows], name="assemble")(
         incoming, sent_tally
     )
-    block_two = passed_along(block, "loop", 2)
-
+
+    block_grad = call(text_kernel, [scalar] * 2 + [whole] * (1 + STOPS), in_vmem(block_shape), name="text_grads")(
+        score_scale_factor, score_shift_term, block, packet, packet_two, packet_relay, packet_swap
+    )
+    block_two = pltpu.with_memory_space_constraint(passed_along(block, "loop", 2), pltpu.VMEM)
     sendback = call(
-        text_kernel, [scalar] * 2 + [whole] * (2 + STOPS), in_vmem(chunks), [staging], name="text_grads", cost=big
-    )(score_scale_factor, score_shift_term, sent_tally, block, packet, packet_two, packet_relay, packet_swap)
+        send_kernel,
+        [whole] * 2,
+        chunks,
+        [staging, leaving, pltpu.SemaphoreType.DMA((PARTS,))],
+        name="send_back",
+        cost=huge,
+        outs=remote,
+    )(sent_tally, block_grad)
     returned = lax.all_to_all(sendback, "grp", split_axis=0, concat_axis=0, tiled=True)
 
     relayed_block = call(relay_kernel, [whole] * 2, in_vmem(block_shape), name="relay_blocks", cost=huge)(
@@ -305,16 +359,19 @@
         image_kernel,
         [scalar] * 2 + [whole] * (1 + STOPS),
         jax.ShapeDtypeStruct((image_rows, features), F32),
+        [pltpu.VMEM((image_rows, features), F32), column_sems],
         name="image_grads",
         cost=big,
+        outs=remote,
     )(score_scale_factor, score_shift_term, packet, block, block_two, block_relay, block_swap)
 
     text_grad = call(
         return_kernel,
         [whole] * 3,
         jax.ShapeDtypeStruct((text_rows, features), F32),
-        [staging, slot_rows],
+        [staging, slot_rows, pltpu.VMEM((text_rows, features), F32), column_sems],
         name="give_back",
+        outs=remote,
     )(returned, listed, sent_tally)
     return (image_grad, text_grad)
 

time: 91.4 us -> 90.9 us (level)
  the two profiles are of different devices: /device:TPU:28 before, /device:TPU:29 now
where the time goes in v3:
time: 90.9 us; the launch traced here: 90.3 us
  starting transfers between devices  54.3 us (60%)
  waiting for transfers between devices  22.1 us (24%)
  Pallas kernels  11.8 us (13%)
  between operations  2.08 us (2%)
    all_to_all x1, starting transfers between devices, local(): lax.all_to_all(outgoing, 'grp', split_axis=0, concat_axis=0, tiled=True)  21.4 us
    ppermute x3, starting transfers between devices, passed_along(): return lax.ppermute(value, axis, pairs)  15.1 us
    all_to_all x1, waiting for transfers between devices, local(): lax.all_to_all(outgoing, 'grp', split_axis=0, concat_axis=0, tiled=True)  12 us
    all_to_all x1, starting transfers between devices, local(): lax.all_to_all(sendback, 'grp', split_axis=0, concat_axis=0, tiled=True)  10 us
    all_to_all x1, waiting for transfers between devices, local(): lax.all_to_all(sendback, 'grp', split_axis=0, concat_axis=0, tiled=True)  8.7 us
    ppermute x2, starting transfers between devices, swapped(): lax.ppermute(value, 'loop', [(source, source ^ 1) for source in range(loo...  4.33 us
    ppermute x1, starting transfers between devices, local(): lax.ppermute(packet, 'loop', [(source, (source - 3 + 2 * (source % 2)) %...  3.43 us
    pallas_call x1, Pallas kernels, local(): call(image_kernel, [scalar] * 2 + [whole] * (1 + STOPS), jax.ShapeDtypeSt...  3.41 us
  transfers between devices with their start and end apart: 8, of which 4 were waited for; matrix products, arithmetic and copies ran while one was open for 0% of the time, Pallas kernels for 9%

profile of v3, /device:TPU:29, one launch (start us, length us, event | category | flops | bytes accessed | tf_op | source)
XLA Modules:
  0.0 90.3 jit_solution(1573103067701409696)
XLA Ops:
  0.6 0.0 copy-start
  0.6 2.2 %prepare.1 = (bf16[272,1152]{1,0:T(8,128)(2,1)S(1)}, bf16[32,54,128]{2,1,0:T(8,128)(2,1)}) custom-call(f32[256,1152]{1,0:T(8,128)} %refs_0_.1, s32[1,256]{1,0:T(1,128)} %bitcast.6, f32[128,1152]{1,0:T(8,128)} %refs_2_.1, s32[6,1,32]{2,1,0:T(1,128)} %bitcast.4), custom_call_target="tpu_custom_call" | custom-call | tf_op jit(solution)/shard_map/prepare/pallas_call | solution.py:299
  2.9 3.1 %collective-permute-start.3 = (bf16[272,1152]{1,0:T(8,128)(2,1)S(1)}, bf16[272,1152]{1,0:T(8,128)(2,1)S(1)}, u32[]{:S(2)}, u32[]{:S(2)}) collective-permute-start(bf16[272,1152]{1,0:T(8,128)(2,1)S(1)} %get-tuple-element.4.packet_ref.refs_0_), channel_id=1, source_target_pairs={{0,960},{32,992},{64,0},{96,32},{128,64},{160,96},{192,128},{224,1... | collective-permute-start | bytes 1880072 | tf_op jit(solution)/shard_map/ppermute | solution.py:20
  5.9 21.4 %all-to-all-start = ((bf16[32,54,128]{2,1,0:T(8,128)(2,1)}), bf16[32,54,128]{2,1,0:T(8,128)(2,1)S(1)}, u32[]{:S(2)}, u32[]{:S(2)}) async-start(bf16[32,54,128]{2,1,0:T(8,128)(2,1)} %get-tuple-element.5), calls=%async_computation | async-start | bytes 917504 | tf_op jit(solution)/shard_map/all_to_all | solution.py:331
  27.4 3.4 %collective-permute-start.4 = (bf16[272,1152]{1,0:T(8,128)(2,1)S(1)}, bf16[272,1152]{1,0:T(8,128)(2,1)S(1)}, u32[]{:S(2)}, u32[]{:S(2)}) collective-permute-start(bf16[272,1152]{1,0:T(8,128)(2,1)S(1)} %get-tuple-element.4.packet_ref.refs_0_), channel_id=1, source_target_pairs={{0,928},{32,0},{64,992},{96,64},{128,32},{160,128},{192,96},{224,1... | collective-permute-start | bytes 1880072 | tf_op jit(solution)/shard_map/ppermute | solution.py:328
  30.8 0.0 collective-permute-done.3.refs_1_
  30.8 1.9 %collective-permute-start.5 = (bf16[272,1152]{1,0:T(8,128)(2,1)S(1)}, bf16[272,1152]{1,0:T(8,128)(2,1)S(1)}, u32[]{:S(2)}, u32[]{:S(2)}) collective-permute-start(bf16[272,1152]{1,0:T(8,128)(2,1)S(1)} %collective-permute-done.3.refs_1_), channel_id=1, source_target_pairs={{0,32},{32,0},{64,96},{96,64},{128,160},{160,128},{192,224},{224,1... | collective-permute-start | bytes 1880072 | tf_op jit(solution)/shard_map/ppermute | solution.py:296
  34.0 12.0 %all-to-all-done.chunks_ref = bf16[32,54,128]{2,1,0:T(8,128)(2,1)S(1)} async-done(((bf16[32,54,128]{2,1,0:T(8,128)(2,1)}), bf16[32,54,128]{2,1,0:T(8,128)(2,1)S(1)}, u32[]{:S(2)}, u32[]{:S(2)}) %all-to-all-start) | async-done | bytes 442400 | tf_op jit(solution)/shard_map/all_to_all | solution.py:331
  46.1 0.0 copy-done
  46.1 0.6 assemble.1.own_ref.refs_0_.block_ref
  46.7 10.2 %collective-permute-start = (bf16[128,1152]{1,0:T(8,128)(2,1)S(1)}, bf16[128,1152]{1,0:T(8,128)(2,1)}, u32[]{:S(2)}, u32[]{:S(2)}) collective-permute-start(bf16[128,1152]{1,0:T(8,128)(2,1)S(1)} %assemble.1.own_ref.refs_0_.block_ref), channel_id=1, source_target_pairs={{0,64},{32,96},{64,128},{96,160},{128,192},{160,224},{192,256},{22... | collective-permute-start | bytes 884744 | tf_op jit(solution)/shard_map/ppermute | solution.py:20
  56.8 0.0 collective-permute-done.4.refs_2_
  56.8 0.0 collective-permute-done.5.refs_3_
  56.8 1.9 %text_grads.1.grad_ref = bf16[128,1152]{1,0:T(8,128)(2,1)S(1)} custom-call(f32[1]{0:T(128)S(6)} %copy.9.scale_ref, f32[1]{0:T(128)S(6)} %copy.10.shift_ref, bf16[128,1152]{1,0:T(8,128)(2,1)S(1)} %assemble.1.own_ref.refs_0_.block_ref, bf16[272,1152]{1,0:T(8,128)(2,1)S(1)} %get-tuple-element.4.packet_ref.refs_0_, ...), custom_call_target="tpu_custom_call" | custom-call | tf_op jit(solution)/shard_map/text_grads/pallas_call | solution.py:338
  58.8 1.3 %send_back.1 = bf16[32,54,128]{2,1,0:T(8,128)(2,1)} custom-call(s32[1,32,32]{2,1,0:T(8,128)S(1)} %copy-done, bf16[128,1152]{1,0:T(8,128)(2,1)S(1)} %text_grads.1.grad_ref), custom_call_target="tpu_custom_call" | custom-call | flops 49999998976 | tf_op jit(solution)/shard_map/send_back/pallas_call | solution.py:342
  60.2 10.0 %all-to-all-start.1 = ((bf16[32,54,128]{2,1,0:T(8,128)(2,1)}), bf16[32,54,128]{2,1,0:T(8,128)(2,1)S(1)}, u32[]{:S(2)}, u32[]{:S(2)}) async-start(bf16[32,54,128]{2,1,0:T(8,128)(2,1)} %send_back.1), calls=%async_computation.1 | async-start | bytes 917504 | tf_op jit(solution)/shard_map/all_to_all | solution.py:351
  70.2 0.0 collective-permute-done.arrived_ref.refs_1_
  70.2 1.0 %relay_blocks.1 = bf16[128,1152]{1,0:T(8,128)(2,1)S(1)} custom-call(bf16[128,1152]{1,0:T(8,128)(2,1)S(1)} %assemble.1.own_ref.refs_0_.block_ref, bf16[128,1152]{1,0:T(8,128)(2,1)} %collective-permute-done.arrived_ref.refs_1_), custom_call_target="tpu_custom_call" | custom-call | flops 49999998976 | tf_op jit(solution)/shard_map/relay_blocks/pallas_call | solution.py:353
  71.2 0.0 copy-start.1
  71.2 1.9 %collective-permute-start.1 = (bf16[128,1152]{1,0:T(8,128)(2,1)S(1)}, bf16[128,1152]{1,0:T(8,128)(2,1)S(1)}, u32[]{:S(2)}, u32[]{:S(2)}) collective-permute-start(bf16[128,1152]{1,0:T(8,128)(2,1)S(1)} %relay_blocks.1), channel_id=1, source_target_pairs={{0,32},{32,64},{64,96},{96,128},{128,160},{160,192},{192,224},{224... | collective-permute-start | bytes 884744 | tf_op jit(solution)/shard_map/ppermute | solution.py:20
  73.1 2.4 %collective-permute-start.2 = (bf16[128,1152]{1,0:T(8,128)(2,1)}, bf16[128,1152]{1,0:T(8,128)(2,1)S(1)}, u32[]{:S(2)}, u32[]{:S(2)}) collective-permute-start(bf16[128,1152]{1,0:T(8,128)(2,1)} %collective-permute-done.arrived_ref.refs_1_), channel_id=1, source_target_pairs={{0,32},{32,0},{64,96},{96,64},{128,160},{160,128},{192,224},{224,1... | collective-permute-start | bytes 884744 | tf_op jit(solution)/shard_map/ppermute | solution.py:296
  75.5 1.2 %collective-permute-done.1.refs_2_ = bf16[128,1152]{1,0:T(8,128)(2,1)S(1)} collective-permute-done((bf16[128,1152]{1,0:T(8,128)(2,1)S(1)}, bf16[128,1152]{1,0:T(8,128)(2,1)S(1)}, u32[]{:S(2)}, u32[]{:S(2)}) %collective-permute-start.1) | collective-permute-done | bytes 294944 | tf_op jit(solution)/shard_map/ppermute | solution.py:20
  76.8 0.2 collective-permute-done.2.refs_3_
  76.9 3.4 %image_grads.1 = f32[256,1152]{1,0:T(8,128)} custom-call(f32[1]{0:T(128)S(6)} %copy.9.scale_ref, f32[1]{0:T(128)S(6)} %copy.10.shift_ref, bf16[272,1152]{1,0:T(8,128)(2,1)S(1)} %get-tuple-element.4.packet_ref.refs_0_, bf16[128,1152]{1,0:T(8,128)(2,1)S(1)} %assemble.1.own_ref.refs_0_.block_ref, bf16[128,1152]{1,0:T(8,128)(2,1)} %collective-permute-done.arrived_ref.refs_1_, ...), custom_call_target="tpu_custom_call" | custom-call | flops 905969664 | bytes 2359296 | tf_op jit(solution)/shard_map/image_grads/pallas_call | solution.py:358
  80.4 8.7 %all-to-all-done.1.chunks_ref = bf16[32,54,128]{2,1,0:T(8,128)(2,1)S(1)} async-done(((bf16[32,54,128]{2,1,0:T(8,128)(2,1)}), bf16[32,54,128]{2,1,0:T(8,128)(2,1)S(1)}, u32[]{:S(2)}, u32[]{:S(2)}) %all-to-all-start.1) | async-done | bytes 442400 | tf_op jit(solution)/shard_map/all_to_all | solution.py:351
  89.1 0.0 copy-done.1
  89.1 1.3 %give_back.1 = f32[128,1152]{1,0:T(8,128)} custom-call(bf16[32,54,128]{2,1,0:T(8,128)(2,1)S(1)} %all-to-all-done.1.chunks_ref, s32[6,1,32]{2,1,0:T(1,128)S(1)} %bitcast.5, s32[1,32,32]{2,1,0:T(8,128)S(1)} %copy-done), custom_call_target="tpu_custom_call" | custom-call | tf_op jit(solution)/shard_map/give_back/pallas_call | solution.py:368
Async XLA Ops:
  0.6 45.4 %copy-start = (s32[1,32,32]{2,1,0:T(8,128)S(1)}, s32[1,32,32]{2,1,0:T(8,128)}, u32[]{:S(2)}) copy-start(s32[1,32,32]{2,1,0:T(8,128)} %tally_ref.5) | copy-start | bytes 12292
  2.9 27.9 %collective-permute-start.3 = (bf16[272,1152]{1,0:T(8,128)(2,1)S(1)}, bf16[272,1152]{1,0:T(8,128)(2,1)S(1)}, u32[]{:S(2)}, u32[]{:S(2)}) collective-permute-start(bf16[272,1152]{1,0:T(8,128)(2,1)S(1)} %get-tuple-element.4.packet_ref.refs_0_), channel_id=1, source_target_pairs={{0,960},{32,992},{64,0},{96,32},{128,64},{160,96},{192,128},{224,1... | collective-permute-start | bytes 1880072 | tf_op jit(solution)/shard_map/ppermute | solution.py:20
  5.9 40.1 %all-to-all-start = ((bf16[32,54,128]{2,1,0:T(8,128)(2,1)}), bf16[32,54,128]{2,1,0:T(8,128)(2,1)S(1)}, u32[]{:S(2)}, u32[]{:S(2)}) async-start(bf16[32,54,128]{2,1,0:T(8,128)(2,1)} %get-tuple-element.5), calls=%async_computation | async-start | bytes 917504 | tf_op jit(solution)/shard_map/all_to_all | solution.py:331
  27.4 29.5 %collective-permute-start.4 = (bf16[272,1152]{1,0:T(8,128)(2,1)S(1)}, bf16[272,1152]{1,0:T(8,128)(2,1)S(1)}, u32[]{:S(2)}, u32[]{:S(2)}) collective-permute-start(bf16[272,1152]{1,0:T(8,128)(2,1)S(1)} %get-tuple-element.4.packet_ref.refs_0_), channel_id=1, source_target_pairs={{0,928},{32,0},{64,992},{96,64},{128,32},{160,128},{192,96},{224,1... | collective-permute-start | bytes 1880072 | tf_op jit(solution)/shard_map/ppermute | solution.py:328
  30.8 26.0 %collective-permute-start.5 = (bf16[272,1152]{1,0:T(8,128)(2,1)S(1)}, bf16[272,1152]{1,0:T(8,128)(2,1)S(1)}, u32[]{:S(2)}, u32[]{:S(2)}) collective-permute-start(bf16[272,1152]{1,0:T(8,128)(2,1)S(1)} %collective-permute-done.3.refs_1_), channel_id=1, source_target_pairs={{0,32},{32,0},{64,96},{96,64},{128,160},{160,128},{192,224},{224,1... | collective-permute-start | bytes 1880072 | tf_op jit(solution)/shard_map/ppermute | solution.py:296
  46.7 23.5 %collective-permute-start = (bf16[128,1152]{1,0:T(8,128)(2,1)S(1)}, bf16[128,1152]{1,0:T(8,128)(2,1)}, u32[]{:S(2)}, u32[]{:S(2)}) collective-permute-start(bf16[128,1152]{1,0:T(8,128)(2,1)S(1)} %assemble.1.own_ref.refs_0_.block_ref), channel_id=1, source_target_pairs={{0,64},{32,96},{64,128},{96,160},{128,192},{160,224},{192,256},{22... | collective-permute-start | bytes 884744 | tf_op jit(solution)/shard_map/ppermute | solution.py:20
  60.2 28.9 %all-to-all-start.1 = ((bf16[32,54,128]{2,1,0:T(8,128)(2,1)}), bf16[32,54,128]{2,1,0:T(8,128)(2,1)S(1)}, u32[]{:S(2)}, u32[]{:S(2)}) async-start(bf16[32,54,128]{2,1,0:T(8,128)(2,1)} %send_back.1), calls=%async_computation.1 | async-start | bytes 917504 | tf_op jit(solution)/shard_map/all_to_all | solution.py:351
  71.2 17.9 %copy-start.1 = (s32[1,1,32,6]{2,1,3,0:T(1,128)S(1)}, s32[1,1,32,6]{2,1,3,0:T(1,128)}, u32[]{:S(2)}) copy-start(s32[1,1,32,6]{2,1,3,0:T(1,128)} %param.9) | copy-start | bytes 2308
  71.2 5.6 %collective-permute-start.1 = (bf16[128,1152]{1,0:T(8,128)(2,1)S(1)}, bf16[128,1152]{1,0:T(8,128)(2,1)S(1)}, u32[]{:S(2)}, u32[]{:S(2)}) collective-permute-start(bf16[128,1152]{1,0:T(8,128)(2,1)S(1)} %relay_blocks.1), channel_id=1, source_target_pairs={{0,32},{32,64},{64,96},{96,128},{128,160},{160,192},{192,224},{224... | collective-permute-start | bytes 884744 | tf_op jit(solution)/shard_map/ppermute | solution.py:20
  73.1 3.8 %collective-permute-start.2 = (bf16[128,1152]{1,0:T(8,128)(2,1)}, bf16[128,1152]{1,0:T(8,128)(2,1)S(1)}, u32[]{:S(2)}, u32[]{:S(2)}) collective-permute-start(bf16[128,1152]{1,0:T(8,128)(2,1)} %collective-permute-done.arrived_ref.refs_1_), channel_id=1, source_target_pairs={{0,32},{32,0},{64,96},{96,64},{128,160},{160,128},{192,224},{224,1... | collective-permute-start | bytes 884744 | tf_op jit(solution)/shard_map/ppermute | solution.py:296

commit v4 on v3

--- a/solution.py
+++ b/solution.py
@@ -146,14 +146,14 @@
         copy.wait()
 
 
-def relay_kernel(own_ref, arrived_ref, out_ref):
+def relay_kernel(passing, own_ref, arrived_ref, out_ref):
     parity = lax.rem(lax.axis_index("loop"), 2)
 
-    @pl.when(parity == 1)
+    @pl.when(parity == passing)
     def _():
         out_ref[...] = arrived_ref[...]
 
-    @pl.when(parity == 0)
+    @pl.when(parity != passing)
     def _():
         out_ref[...] = own_ref[...]
 
@@ -291,6 +291,12 @@
 
     def prepare_body(*refs):
         prepare_kernel(loop_count, group_count, *refs)
+
+    def keep_even(*refs):
+        relay_kernel(0, *refs)
+
+    def keep_odd(*refs):
+        relay_kernel(1, *refs)
 
     def swapped(value):
         return lax.ppermute(value, "loop", [(source, source ^ 1) for source in range(loop_count)])
@@ -325,11 +331,10 @@
     )
 
     packet_two = passed_along(packet, "loop", -2)
-    packet_relay = lax.ppermute(
-        packet, "loop", [(source, (source - 3 + 2 * (source % 2)) % loop_count) for source in range(loop_count)]
-    )
     incoming = lax.all_to_all(outgoing, "grp", split_axis=0, concat_axis=0, tiled=True)
     packet_swap = swapped(packet_two)
+    relayed = call(keep_even, [whole] * 2, in_vmem(packet_shape), name="relay_images")(packet, packet_two)
+    packet_relay = passed_along(relayed, "loop", -1)
 
     block = call(assemble_kernel, [whole] * 2, in_vmem(block_shape), [staging, slot_rows], name="assemble")(
         incoming, sent_tally
@@ -350,7 +355,7 @@
     )(sent_tally, block_grad)
     returned = lax.all_to_all(sendback, "grp", split_axis=0, concat_axis=0, tiled=True)
 
-    relayed_block = call(relay_kernel, [whole] * 2, in_vmem(block_shape), name="relay_blocks", cost=huge)(
+    relayed_block = call(keep_odd, [whole] * 2, in_vmem(block_shape), name="relay_blocks", cost=huge)(
         block, block_two
     )
     block_relay = passed_along(relayed_block, "loop", 1)

time: 90.9 us -> 87.3 us (0.960)
  the two profiles are of different devices: /device:TPU:29 before, /device:TPU:159 now
where the time goes in v4:
time: 87.3 us; the launch traced here: 86.8 us
  starting transfers between devices  49.4 us (57%)
  waiting for transfers between devices  24.5 us (28%)
  Pallas kernels  10.7 us (12%)
  between operations  2.08 us (2%)
    all_to_all x1, starting transfers between devices, local(): lax.all_to_all(outgoing, 'grp', split_axis=0, concat_axis=0, tiled=True)  20.6 us
    all_to_all x1, starting transfers between devices, local(): lax.all_to_all(sendback, 'grp', split_axis=0, concat_axis=0, tiled=True)  14.2 us
    all_to_all x1, waiting for transfers between devices, local(): lax.all_to_all(outgoing, 'grp', split_axis=0, concat_axis=0, tiled=True)  12.6 us
    ppermute x4, starting transfers between devices, passed_along(): return lax.ppermute(value, axis, pairs)  10.7 us
    all_to_all x1, waiting for transfers between devices, local(): lax.all_to_all(sendback, 'grp', split_axis=0, concat_axis=0, tiled=True)  9.57 us
    ppermute x2, starting transfers between devices, swapped(): lax.ppermute(value, 'loop', [(source, source ^ 1) for source in range(loo...  3.91 us
    pallas_call x1, Pallas kernels, local(): call(image_kernel, [scalar] * 2 + [whole] * (1 + STOPS), jax.ShapeDtypeSt...  2.45 us
    ppermute x4, waiting for transfers between devices, passed_along(): return lax.ppermute(value, axis, pairs)  2.37 us
  transfers between devices with their start and end apart: 8, of which 3 were waited for; matrix products, arithmetic and copies ran while one was open for 0% of the time, Pallas kernels for 8%

profile of v4, /device:TPU:159, one launch (start us, length us, event | category | flops | bytes accessed | tf_op | source)
XLA Modules:
  0.0 86.8 jit_solution(7019331586468901097)
XLA Ops:
  0.6 2.2 %prepare.1 = (bf16[272,1152]{1,0:T(8,128)(2,1)S(1)}, bf16[32,54,128]{2,1,0:T(8,128)(2,1)}) custom-call(f32[256,1152]{1,0:T(8,128)} %refs_0_.1, s32[1,256]{1,0:T(1,128)} %bitcast.6, f32[128,1152]{1,0:T(8,128)} %refs_2_.1, s32[6,1,32]{2,1,0:T(1,128)} %bitcast.4), custom_call_target="tpu_custom_call" | custom-call | tf_op jit(solution)/shard_map/prepare/pallas_call | solution.py:305
  2.9 3.1 %collective-permute-start.3 = (bf16[272,1152]{1,0:T(8,128)(2,1)S(1)}, bf16[272,1152]{1,0:T(8,128)(2,1)S(1)}, u32[]{:S(2)}, u32[]{:S(2)}) collective-permute-start(bf16[272,1152]{1,0:T(8,128)(2,1)S(1)} %get-tuple-element.4.packet_ref.refs_0_), channel_id=1, source_target_pairs={{0,960},{32,992},{64,0},{96,32},{128,64},{160,96},{192,128},{224,1... | collective-permute-start | bytes 1880072 | tf_op jit(solution)/shard_map/ppermute | solution.py:20
  5.9 0.0 copy-start
  5.9 20.6 %all-to-all-start = ((bf16[32,54,128]{2,1,0:T(8,128)(2,1)}), bf16[32,54,128]{2,1,0:T(8,128)(2,1)S(1)}, u32[]{:S(2)}, u32[]{:S(2)}) async-start(bf16[32,54,128]{2,1,0:T(8,128)(2,1)} %get-tuple-element.5), calls=%async_computation | async-start | bytes 917504 | tf_op jit(solution)/shard_map/all_to_all | solution.py:334
  26.5 0.0 collective-permute-done.3.refs_1_
  26.5 0.9 %relay_images.1 = bf16[272,1152]{1,0:T(8,128)(2,1)} custom-call(bf16[272,1152]{1,0:T(8,128)(2,1)S(1)} %get-tuple-element.4.packet_ref.refs_0_, bf16[272,1152]{1,0:T(8,128)(2,1)S(1)} %collective-permute-done.3.refs_1_), custom_call_target="tpu_custom_call" | custom-call | tf_op jit(solution)/shard_map/relay_images/pallas_call | solution.py:336
  27.4 3.4 %collective-permute-start.4 = (bf16[272,1152]{1,0:T(8,128)(2,1)}, bf16[272,1152]{1,0:T(8,128)(2,1)S(1)}, u32[]{:S(2)}, u32[]{:S(2)}) collective-permute-start(bf16[272,1152]{1,0:T(8,128)(2,1)} %relay_images.1), channel_id=1, source_target_pairs={{0,992},{32,0},{64,32},{96,64},{128,96},{160,128},{192,160},{224,1... | collective-permute-start | bytes 1880072 | tf_op jit(solution)/shard_map/ppermute | solution.py:20
  30.8 1.9 %collective-permute-start.5 = (bf16[272,1152]{1,0:T(8,128)(2,1)S(1)}, bf16[272,1152]{1,0:T(8,128)(2,1)S(1)}, u32[]{:S(2)}, u32[]{:S(2)}) collective-permute-start(bf16[272,1152]{1,0:T(8,128)(2,1)S(1)} %collective-permute-done.3.refs_1_), channel_id=1, source_target_pairs={{0,32},{32,0},{64,96},{96,64},{128,160},{160,128},{192,224},{224,1... | collective-permute-start | bytes 1880072 | tf_op jit(solution)/shard_map/ppermute | solution.py:302
  34.1 12.6 %all-to-all-done.chunks_ref = bf16[32,54,128]{2,1,0:T(8,128)(2,1)S(1)} async-done(((bf16[32,54,128]{2,1,0:T(8,128)(2,1)}), bf16[32,54,128]{2,1,0:T(8,128)(2,1)S(1)}, u32[]{:S(2)}, u32[]{:S(2)}) %all-to-all-start) | async-done | bytes 442400 | tf_op jit(solution)/shard_map/all_to_all | solution.py:334
  46.7 0.0 copy-done
  46.7 0.6 assemble.1.refs_0_.block_ref
  47.3 1.9 %collective-permute-start = (bf16[128,1152]{1,0:T(8,128)(2,1)S(1)}, bf16[128,1152]{1,0:T(8,128)(2,1)S(1)}, u32[]{:S(2)}, u32[]{:S(2)}) collective-permute-start(bf16[128,1152]{1,0:T(8,128)(2,1)S(1)} %assemble.1.refs_0_.block_ref), channel_id=1, source_target_pairs={{0,64},{32,96},{64,128},{96,160},{128,192},{160,224},{192,256},{22... | collective-permute-start | bytes 884744 | tf_op jit(solution)/shard_map/ppermute | solution.py:20
  49.2 0.0 collective-permute-done.4.refs_2_
  49.2 0.0 collective-permute-done.5.refs_3_
  49.2 1.9 %text_grads.1.grad_ref = bf16[128,1152]{1,0:T(8,128)(2,1)S(1)} custom-call(f32[1]{0:T(128)S(6)} %copy.9.scale_ref, f32[1]{0:T(128)S(6)} %copy.10.shift_ref, bf16[128,1152]{1,0:T(8,128)(2,1)S(1)} %assemble.1.refs_0_.block_ref, bf16[272,1152]{1,0:T(8,128)(2,1)S(1)} %get-tuple-element.4.packet_ref.refs_0_, ...), custom_call_target="tpu_custom_call" | custom-call | tf_op jit(solution)/shard_map/text_grads/pallas_call | solution.py:343
  51.2 1.4 %send_back.1 = bf16[32,54,128]{2,1,0:T(8,128)(2,1)} custom-call(s32[1,32,32]{2,1,0:T(8,128)S(1)} %copy-done, bf16[128,1152]{1,0:T(8,128)(2,1)S(1)} %text_grads.1.grad_ref), custom_call_target="tpu_custom_call" | custom-call | flops 49999998976 | tf_op jit(solution)/shard_map/send_back/pallas_call | solution.py:347
  52.5 14.2 %all-to-all-start.1 = ((bf16[32,54,128]{2,1,0:T(8,128)(2,1)}), bf16[32,54,128]{2,1,0:T(8,128)(2,1)S(1)}, u32[]{:S(2)}, u32[]{:S(2)}) async-start(bf16[32,54,128]{2,1,0:T(8,128)(2,1)} %send_back.1), calls=%async_computation.1 | async-start | bytes 917504 | tf_op jit(solution)/shard_map/all_to_all | solution.py:356
  66.7 0.0 collective-permute-done.refs_1_
  66.8 0.0 copy-start.1
  66.8 2.4 %collective-permute-start.1 = (bf16[128,1152]{1,0:T(8,128)(2,1)S(1)}, bf16[128,1152]{1,0:T(8,128)(2,1)S(1)}, u32[]{:S(2)}, u32[]{:S(2)}) collective-permute-start(bf16[128,1152]{1,0:T(8,128)(2,1)S(1)} %relay_blocks.1), channel_id=1, source_target_pairs={{0,32},{32,64},{64,96},{96,128},{128,160},{160,192},{192,224},{224... | collective-permute-start | bytes 884744 | tf_op jit(solution)/shard_map/ppermute | solution.py:20
  69.2 2.0 %collective-permute-start.2 = (bf16[128,1152]{1,0:T(8,128)(2,1)S(1)}, bf16[128,1152]{1,0:T(8,128)(2,1)S(1)}, u32[]{:S(2)}, u32[]{:S(2)}) collective-permute-start(bf16[128,1152]{1,0:T(8,128)(2,1)S(1)} %collective-permute-done.refs_1_), channel_id=1, source_target_pairs={{0,32},{32,0},{64,96},{96,64},{128,160},{160,128},{192,224},{224,1... | collective-permute-start | bytes 884744 | tf_op jit(solution)/shard_map/ppermute | solution.py:302
  71.1 2.4 %collective-permute-done.1.refs_2_ = bf16[128,1152]{1,0:T(8,128)(2,1)S(1)} collective-permute-done((bf16[128,1152]{1,0:T(8,128)(2,1)S(1)}, bf16[128,1152]{1,0:T(8,128)(2,1)S(1)}, u32[]{:S(2)}, u32[]{:S(2)}) %collective-permute-start.1) | collective-permute-done | bytes 294944 | tf_op jit(solution)/shard_map/ppermute | solution.py:20
  73.5 0.0 collective-permute-done.2.refs_3_
  73.5 2.4 %image_grads.1 = f32[256,1152]{1,0:T(8,128)} custom-call(f32[1]{0:T(128)S(6)} %copy.9.scale_ref, f32[1]{0:T(128)S(6)} %copy.10.shift_ref, bf16[272,1152]{1,0:T(8,128)(2,1)S(1)} %get-tuple-element.4.packet_ref.refs_0_, bf16[128,1152]{1,0:T(8,128)(2,1)S(1)} %assemble.1.refs_0_.block_ref, bf16[128,1152]{1,0:T(8,128)(2,1)S(1)} %collective-permute-done.refs_1_, ...), custom_call_target="tpu_custom_call" | custom-call | flops 905969664 | bytes 2359296 | tf_op jit(solution)/shard_map/image_grads/pallas_call | solution.py:363
  76.0 9.6 %all-to-all-done.1.chunks_ref = bf16[32,54,128]{2,1,0:T(8,128)(2,1)S(1)} async-done(((bf16[32,54,128]{2,1,0:T(8,128)(2,1)}), bf16[32,54,128]{2,1,0:T(8,128)(2,1)S(1)}, u32[]{:S(2)}, u32[]{:S(2)}) %all-to-all-start.1) | async-done | bytes 442400 | tf_op jit(solution)/shard_map/all_to_all | solution.py:356
  85.5 0.0 copy-done.1
  85.5 1.3 %give_back.1 = f32[128,1152]{1,0:T(8,128)} custom-call(bf16[32,54,128]{2,1,0:T(8,128)(2,1)S(1)} %all-to-all-done.1.chunks_ref, s32[6,1,32]{2,1,0:T(1,128)S(1)} %bitcast.5, s32[1,32,32]{2,1,0:T(8,128)S(1)} %copy-done), custom_call_target="tpu_custom_call" | custom-call | tf_op jit(solution)/shard_map/give_back/pallas_call | solution.py:373
  (1 shorter events, 0.0 us)
Async XLA Ops:
  2.9 23.7 %collective-permute-start.3 = (bf16[272,1152]{1,0:T(8,128)(2,1)S(1)}, bf16[272,1152]{1,0:T(8,128)(2,1)S(1)}, u32[]{:S(2)}, u32[]{:S(2)}) collective-permute-start(bf16[272,1152]{1,0:T(8,128)(2,1)S(1)} %get-tuple-element.4.packet_ref.refs_0_), channel_id=1, source_target_pairs={{0,960},{32,992},{64,0},{96,32},{128,64},{160,96},{192,128},{224,1... | collective-permute-start | bytes 1880072 | tf_op jit(solution)/shard_map/ppermute | solution.py:20
  5.9 40.8 %copy-start = (s32[1,32,32]{2,1,0:T(8,128)S(1)}, s32[1,32,32]{2,1,0:T(8,128)}, u32[]{:S(2)}) copy-start(s32[1,32,32]{2,1,0:T(8,128)} %tally_ref.5) | copy-start | bytes 12292
  5.9 40.7 %all-to-all-start = ((bf16[32,54,128]{2,1,0:T(8,128)(2,1)}), bf16[32,54,128]{2,1,0:T(8,128)(2,1)S(1)}, u32[]{:S(2)}, u32[]{:S(2)}) async-start(bf16[32,54,128]{2,1,0:T(8,128)(2,1)} %get-tuple-element.5), calls=%async_computation | async-start | bytes 917504 | tf_op jit(solution)/shard_map/all_to_all | solution.py:334
  27.4 21.8 %collective-permute-start.4 = (bf16[272,1152]{1,0:T(8,128)(2,1)}, bf16[272,1152]{1,0:T(8,128)(2,1)S(1)}, u32[]{:S(2)}, u32[]{:S(2)}) collective-permute-start(bf16[272,1152]{1,0:T(8,128)(2,1)} %relay_images.1), channel_id=1, source_target_pairs={{0,992},{32,0},{64,32},{96,64},{128,96},{160,128},{192,160},{224,1... | collective-permute-start | bytes 1880072 | tf_op jit(solution)/shard_map/ppermute | solution.py:20
  30.8 18.4 %collective-permute-start.5 = (bf16[272,1152]{1,0:T(8,128)(2,1)S(1)}, bf16[272,1152]{1,0:T(8,128)(2,1)S(1)}, u32[]{:S(2)}, u32[]{:S(2)}) collective-permute-start(bf16[272,1152]{1,0:T(8,128)(2,1)S(1)} %collective-permute-done.3.refs_1_), channel_id=1, source_target_pairs={{0,32},{32,0},{64,96},{96,64},{128,160},{160,128},{192,224},{224,1... | collective-permute-start | bytes 1880072 | tf_op jit(solution)/shard_map/ppermute | solution.py:302
  47.3 19.4 %collective-permute-start = (bf16[128,1152]{1,0:T(8,128)(2,1)S(1)}, bf16[128,1152]{1,0:T(8,128)(2,1)S(1)}, u32[]{:S(2)}, u32[]{:S(2)}) collective-permute-start(bf16[128,1152]{1,0:T(8,128)(2,1)S(1)} %assemble.1.refs_0_.block_ref), channel_id=1, source_target_pairs={{0,64},{32,96},{64,128},{96,160},{128,192},{160,224},{192,256},{22... | collective-permute-start | bytes 884744 | tf_op jit(solution)/shard_map/ppermute | solution.py:20
  52.5 33.0 %all-to-all-start.1 = ((bf16[32,54,128]{2,1,0:T(8,128)(2,1)}), bf16[32,54,128]{2,1,0:T(8,128)(2,1)S(1)}, u32[]{:S(2)}, u32[]{:S(2)}) async-start(bf16[32,54,128]{2,1,0:T(8,128)(2,1)} %send_back.1), calls=%async_computation.1 | async-start | bytes 917504 | tf_op jit(solution)/shard_map/all_to_all | solution.py:356
  66.8 18.7 %copy-start.1 = (s32[1,1,32,6]{2,1,3,0:T(1,128)S(1)}, s32[1,1,32,6]{2,1,3,0:T(1,128)}, u32[]{:S(2)}) copy-start(s32[1,1,32,6]{2,1,3,0:T(1,128)} %param.9) | copy-start | bytes 2308
  66.8 6.7 %collective-permute-start.1 = (bf16[128,1152]{1,0:T(8,128)(2,1)S(1)}, bf16[128,1152]{1,0:T(8,128)(2,1)S(1)}, u32[]{:S(2)}, u32[]{:S(2)}) collective-permute-start(bf16[128,1152]{1,0:T(8,128)(2,1)S(1)} %relay_blocks.1), channel_id=1, source_target_pairs={{0,32},{32,64},{64,96},{96,128},{128,160},{160,192},{192,224},{224... | collective-permute-start | bytes 884744 | tf_op jit(solution)/shard_map/ppermute | solution.py:20
  69.2 4.3 %collective-permute-start.2 = (bf16[128,1152]{1,0:T(8,128)(2,1)S(1)}, bf16[128,1152]{1,0:T(8,128)(2,1)S(1)}, u32[]{:S(2)}, u32[]{:S(2)}) collective-permute-start(bf16[128,1152]{1,0:T(8,128)(2,1)S(1)} %collective-permute-done.refs_1_), channel_id=1, source_target_pairs={{0,32},{32,0},{64,96},{96,64},{128,160},{160,128},{192,224},{224,1... | collective-permute-start | bytes 884744 | tf_op jit(solution)/shard_map/ppermute | solution.py:302

commit v5 on v4

--- a/solution.py
+++ b/solution.py
@@ -173,12 +173,16 @@
     text = block_ref[...]
     rows = packets[0].shape[0] - AUX_ROWS
     odd = lax.rem(lax.axis_index("loop"), 2)
-    total = jnp.zeros(text.shape, F32)
-    for stop, packet in zip((0, 2, 1 + 2 * odd, 3 - 2 * odd), packets):
-        image = packet[0:rows, :]
-        slopes = slopes_for(text, image, places_of(packet, stop), scale, shift)
-        total = total + jnp.dot(slopes, image, preferred_element_type=F32)
-    grad_ref[...] = total.astype(BF16)
+    slopes = [
+        slopes_for(text, packet[0:rows, :], places_of(packet, stop), scale, shift)
+        for stop, packet in zip((0, 2, 1 + 2 * odd, 3 - 2 * odd), packets)
+    ]
+    for start in range(0, text.shape[1], WIDTH):
+        total = None
+        for slope, packet in zip(slopes, packets):
+            term = jnp.dot(slope, packet[0:rows, start : start + WIDTH], preferred_element_type=F32)
+            total = term if total is None else total + term
+        grad_ref[:, start : start + WIDTH] = total.astype(BF16)
 
 
 def send_kernel(tally_ref, grad_ref, chunks_hbm, staging, chunks_ref, sent):
@@ -284,7 +288,7 @@
             in_specs=in_specs,
             out_specs=jax.tree.map(lambda _: whole, out_shape) if outs is None else outs,
             scratch_shapes=list(scratch),
-            compiler_params=pltpu.CompilerParams(vmem_limit_bytes=24 * 1024 * 1024),
+            compiler_params=pltpu.CompilerParams(vmem_limit_bytes=12 * 1024 * 1024),
             name=name,
             cost_estimate=cost,
         )

time: 87.3 us -> 86.8 us (level)
  no operation moved by 1% of the time
where the time goes in v5:
time: 86.8 us; the launch traced here: 86.3 us
  starting transfers between devices  49.4 us (57%)
  waiting for transfers between devices  24.5 us (28%)
  Pallas kernels  10.2 us (12%)
  between operations  2.08 us (2%)
    all_to_all x1, starting transfers between devices, local(): lax.all_to_all(outgoing, 'grp', split_axis=0, concat_axis=0, tiled=True)  20.6 us
    all_to_all x1, starting transfers between devices, local(): lax.all_to_all(sendback, 'grp', split_axis=0, concat_axis=0, tiled=True)  14.2 us
    all_to_all x1, waiting for transfers between devices, local(): lax.all_to_all(outgoing, 'grp', split_axis=0, concat_axis=0, tiled=True)  12.6 us
    ppermute x4, starting transfers between devices, passed_along(): return lax.ppermute(value, axis, pairs)  10.7 us
    all_to_all x1, waiting for transfers between devices, local(): lax.all_to_all(sendback, 'grp', split_axis=0, concat_axis=0, tiled=True)  9.57 us
    ppermute x2, starting transfers between devices, swapped(): lax.ppermute(value, 'loop', [(source, source ^ 1) for source in range(loo...  3.91 us
    pallas_call x1, Pallas kernels, local(): call(image_kernel, [scalar] * 2 + [whole] * (1 + STOPS), jax.ShapeDtypeSt...  2.45 us
    ppermute x4, waiting for transfers between devices, passed_along(): return lax.ppermute(value, axis, pairs)  2.36 us
  transfers between devices with their start and end apart: 8, of which 3 were waited for; matrix products, arithmetic and copies ran while one was open for 0% of the time, Pallas kernels for 8%

profile of v5, /device:TPU:159, one launch (start us, length us, event | category | flops | bytes accessed | tf_op | source)
XLA Modules:
  0.0 86.3 jit_solution(13815741758559842124)
XLA Ops:
  0.6 2.2 %prepare.1 = (bf16[272,1152]{1,0:T(8,128)(2,1)S(1)}, bf16[32,54,128]{2,1,0:T(8,128)(2,1)}) custom-call(f32[256,1152]{1,0:T(8,128)} %refs_0_.1, s32[1,256]{1,0:T(1,128)} %bitcast.6, f32[128,1152]{1,0:T(8,128)} %refs_2_.1, s32[6,1,32]{2,1,0:T(1,128)} %bitcast.4), custom_call_target="tpu_custom_call" | custom-call | tf_op jit(solution)/shard_map/prepare/pallas_call | solution.py:309
  2.9 3.1 %collective-permute-start.3 = (bf16[272,1152]{1,0:T(8,128)(2,1)S(1)}, bf16[272,1152]{1,0:T(8,128)(2,1)S(1)}, u32[]{:S(2)}, u32[]{:S(2)}) collective-permute-start(bf16[272,1152]{1,0:T(8,128)(2,1)S(1)} %get-tuple-element.4.packet_ref.refs_0_), channel_id=1, source_target_pairs={{0,960},{32,992},{64,0},{96,32},{128,64},{160,96},{192,128},{224,1... | collective-permute-start | bytes 1880072 | tf_op jit(solution)/shard_map/ppermute | solution.py:20
  5.9 0.0 copy-start
  5.9 20.6 %all-to-all-start = ((bf16[32,54,128]{2,1,0:T(8,128)(2,1)}), bf16[32,54,128]{2,1,0:T(8,128)(2,1)S(1)}, u32[]{:S(2)}, u32[]{:S(2)}) async-start(bf16[32,54,128]{2,1,0:T(8,128)(2,1)} %get-tuple-element.5), calls=%async_computation | async-start | bytes 917504 | tf_op jit(solution)/shard_map/all_to_all | solution.py:338
  26.5 0.0 collective-permute-done.3.refs_1_
  26.5 0.9 %relay_images.1 = bf16[272,1152]{1,0:T(8,128)(2,1)} custom-call(bf16[272,1152]{1,0:T(8,128)(2,1)S(1)} %get-tuple-element.4.packet_ref.refs_0_, bf16[272,1152]{1,0:T(8,128)(2,1)S(1)} %collective-permute-done.3.refs_1_), custom_call_target="tpu_custom_call" | custom-call | tf_op jit(solution)/shard_map/relay_images/pallas_call | solution.py:340
  27.4 3.4 %collective-permute-start.4 = (bf16[272,1152]{1,0:T(8,128)(2,1)}, bf16[272,1152]{1,0:T(8,128)(2,1)S(1)}, u32[]{:S(2)}, u32[]{:S(2)}) collective-permute-start(bf16[272,1152]{1,0:T(8,128)(2,1)} %relay_images.1), channel_id=1, source_target_pairs={{0,992},{32,0},{64,32},{96,64},{128,96},{160,128},{192,160},{224,1... | collective-permute-start | bytes 1880072 | tf_op jit(solution)/shard_map/ppermute | solution.py:20
  30.8 1.9 %collective-permute-start.5 = (bf16[272,1152]{1,0:T(8,128)(2,1)S(1)}, bf16[272,1152]{1,0:T(8,128)(2,1)S(1)}, u32[]{:S(2)}, u32[]{:S(2)}) collective-permute-start(bf16[272,1152]{1,0:T(8,128)(2,1)S(1)} %collective-permute-done.3.refs_1_), channel_id=1, source_target_pairs={{0,32},{32,0},{64,96},{96,64},{128,160},{160,128},{192,224},{224,1... | collective-permute-start | bytes 1880072 | tf_op jit(solution)/shard_map/ppermute | solution.py:306
  34.1 12.6 %all-to-all-done.chunks_ref = bf16[32,54,128]{2,1,0:T(8,128)(2,1)S(1)} async-done(((bf16[32,54,128]{2,1,0:T(8,128)(2,1)}), bf16[32,54,128]{2,1,0:T(8,128)(2,1)S(1)}, u32[]{:S(2)}, u32[]{:S(2)}) %all-to-all-start) | async-done | bytes 442400 | tf_op jit(solution)/shard_map/all_to_all | solution.py:338
  46.7 0.0 copy-done
  46.7 0.6 assemble.1.refs_0_.block_ref
  47.3 1.9 %collective-permute-start = (bf16[128,1152]{1,0:T(8,128)(2,1)S(1)}, bf16[128,1152]{1,0:T(8,128)(2,1)S(1)}, u32[]{:S(2)}, u32[]{:S(2)}) collective-permute-start(bf16[128,1152]{1,0:T(8,128)(2,1)S(1)} %assemble.1.refs_0_.block_ref), channel_id=1, source_target_pairs={{0,64},{32,96},{64,128},{96,160},{128,192},{160,224},{192,256},{22... | collective-permute-start | bytes 884744 | tf_op jit(solution)/shard_map/ppermute | solution.py:20
  49.2 0.0 collective-permute-done.4.refs_2_
  49.2 0.0 collective-permute-done.5.refs_3_
  49.2 1.4 %text_grads.1.grad_ref = bf16[128,1152]{1,0:T(8,128)(2,1)S(1)} custom-call(f32[1]{0:T(128)S(6)} %copy.9.scale_ref, f32[1]{0:T(128)S(6)} %copy.10.shift_ref, bf16[128,1152]{1,0:T(8,128)(2,1)S(1)} %assemble.1.refs_0_.block_ref, bf16[272,1152]{1,0:T(8,128)(2,1)S(1)} %get-tuple-element.4.packet_ref.refs_0_, ...), custom_call_target="tpu_custom_call" | custom-call | tf_op jit(solution)/shard_map/text_grads/pallas_call | solution.py:347
  50.7 1.3 %send_back.1 = bf16[32,54,128]{2,1,0:T(8,128)(2,1)} custom-call(s32[1,32,32]{2,1,0:T(8,128)S(1)} %copy-done, bf16[128,1152]{1,0:T(8,128)(2,1)S(1)} %text_grads.1.grad_ref), custom_call_target="tpu_custom_call" | custom-call | flops 49999998976 | tf_op jit(solution)/shard_map/send_back/pallas_call | solution.py:351
  52.0 14.2 %all-to-all-start.1 = ((bf16[32,54,128]{2,1,0:T(8,128)(2,1)}), bf16[32,54,128]{2,1,0:T(8,128)(2,1)S(1)}, u32[]{:S(2)}, u32[]{:S(2)}) async-start(bf16[32,54,128]{2,1,0:T(8,128)(2,1)} %send_back.1), calls=%async_computation.1 | async-start | bytes 917504 | tf_op jit(solution)/shard_map/all_to_all | solution.py:360
  66.2 0.0 collective-permute-done.refs_1_
  66.3 0.0 copy-start.1
  66.3 2.4 %collective-permute-start.1 = (bf16[128,1152]{1,0:T(8,128)(2,1)S(1)}, bf16[128,1152]{1,0:T(8,128)(2,1)S(1)}, u32[]{:S(2)}, u32[]{:S(2)}) collective-permute-start(bf16[128,1152]{1,0:T(8,128)(2,1)S(1)} %relay_blocks.1), channel_id=1, source_target_pairs={{0,32},{32,64},{64,96},{96,128},{128,160},{160,192},{192,224},{224... | collective-permute-start | bytes 884744 | tf_op jit(solution)/shard_map/ppermute | solution.py:20
  68.7 2.0 %collective-permute-start.2 = (bf16[128,1152]{1,0:T(8,128)(2,1)S(1)}, bf16[128,1152]{1,0:T(8,128)(2,1)S(1)}, u32[]{:S(2)}, u32[]{:S(2)}) collective-permute-start(bf16[128,1152]{1,0:T(8,128)(2,1)S(1)} %collective-permute-done.refs_1_), channel_id=1, source_target_pairs={{0,32},{32,0},{64,96},{96,64},{128,160},{160,128},{192,224},{224,1... | collective-permute-start | bytes 884744 | tf_op jit(solution)/shard_map/ppermute | solution.py:306
  70.6 2.4 %collective-permute-done.1.refs_2_ = bf16[128,1152]{1,0:T(8,128)(2,1)S(1)} collective-permute-done((bf16[128,1152]{1,0:T(8,128)(2,1)S(1)}, bf16[128,1152]{1,0:T(8,128)(2,1)S(1)}, u32[]{:S(2)}, u32[]{:S(2)}) %collective-permute-start.1) | collective-permute-done | bytes 294944 | tf_op jit(solution)/shard_map/ppermute | solution.py:20
  73.0 0.0 collective-permute-done.2.refs_3_
  73.0 2.5 %image_grads.1 = f32[256,1152]{1,0:T(8,128)} custom-call(f32[1]{0:T(128)S(6)} %copy.9.scale_ref, f32[1]{0:T(128)S(6)} %copy.10.shift_ref, bf16[272,1152]{1,0:T(8,128)(2,1)S(1)} %get-tuple-element.4.packet_ref.refs_0_, bf16[128,1152]{1,0:T(8,128)(2,1)S(1)} %assemble.1.refs_0_.block_ref, bf16[128,1152]{1,0:T(8,128)(2,1)S(1)} %collective-permute-done.refs_1_, ...), custom_call_target="tpu_custom_call" | custom-call | flops 905969664 | bytes 2359296 | tf_op jit(solution)/shard_map/image_grads/pallas_call | solution.py:367
  75.4 9.6 %all-to-all-done.1.chunks_ref = bf16[32,54,128]{2,1,0:T(8,128)(2,1)S(1)} async-done(((bf16[32,54,128]{2,1,0:T(8,128)(2,1)}), bf16[32,54,128]{2,1,0:T(8,128)(2,1)S(1)}, u32[]{:S(2)}, u32[]{:S(2)}) %all-to-all-start.1) | async-done | bytes 442400 | tf_op jit(solution)/shard_map/all_to_all | solution.py:360
  85.0 0.0 copy-done.1
  85.0 1.3 %give_back.1 = f32[128,1152]{1,0:T(8,128)} custom-call(bf16[32,54,128]{2,1,0:T(8,128)(2,1)S(1)} %all-to-all-done.1.chunks_ref, s32[6,1,32]{2,1,0:T(1,128)S(1)} %bitcast.5, s32[1,32,32]{2,1,0:T(8,128)S(1)} %copy-done), custom_call_target="tpu_custom_call" | custom-call | tf_op jit(solution)/shard_map/give_back/pallas_call | solution.py:377
  (1 shorter events, 0.0 us)
Async XLA Ops:
  2.9 23.7 %collective-permute-start.3 = (bf16[272,1152]{1,0:T(8,128)(2,1)S(1)}, bf16[272,1152]{1,0:T(8,128)(2,1)S(1)}, u32[]{:S(2)}, u32[]{:S(2)}) collective-permute-start(bf16[272,1152]{1,0:T(8,128)(2,1)S(1)} %get-tuple-element.4.packet_ref.refs_0_), channel_id=1, source_target_pairs={{0,960},{32,992},{64,0},{96,32},{128,64},{160,96},{192,128},{224,1... | collective-permute-start | bytes 1880072 | tf_op jit(solution)/shard_map/ppermute | solution.py:20
  5.9 40.8 %copy-start = (s32[1,32,32]{2,1,0:T(8,128)S(1)}, s32[1,32,32]{2,1,0:T(8,128)}, u32[]{:S(2)}) copy-start(s32[1,32,32]{2,1,0:T(8,128)} %tally_ref.5) | copy-start | bytes 12292
  5.9 40.7 %all-to-all-start = ((bf16[32,54,128]{2,1,0:T(8,128)(2,1)}), bf16[32,54,128]{2,1,0:T(8,128)(2,1)S(1)}, u32[]{:S(2)}, u32[]{:S(2)}) async-start(bf16[32,54,128]{2,1,0:T(8,128)(2,1)} %get-tuple-element.5), calls=%async_computation | async-start | bytes 917504 | tf_op jit(solution)/shard_map/all_to_all | solution.py:338
  27.4 21.8 %collective-permute-start.4 = (bf16[272,1152]{1,0:T(8,128)(2,1)}, bf16[272,1152]{1,0:T(8,128)(2,1)S(1)}, u32[]{:S(2)}, u32[]{:S(2)}) collective-permute-start(bf16[272,1152]{1,0:T(8,128)(2,1)} %relay_images.1), channel_id=1, source_target_pairs={{0,992},{32,0},{64,32},{96,64},{128,96},{160,128},{192,160},{224,1... | collective-permute-start | bytes 1880072 | tf_op jit(solution)/shard_map/ppermute | solution.py:20
  30.8 18.4 %collective-permute-start.5 = (bf16[272,1152]{1,0:T(8,128)(2,1)S(1)}, bf16[272,1152]{1,0:T(8,128)(2,1)S(1)}, u32[]{:S(2)}, u32[]{:S(2)}) collective-permute-start(bf16[272,1152]{1,0:T(8,128)(2,1)S(1)} %collective-permute-done.3.refs_1_), channel_id=1, source_target_pairs={{0,32},{32,0},{64,96},{96,64},{128,160},{160,128},{192,224},{224,1... | collective-permute-start | bytes 1880072 | tf_op jit(solution)/shard_map/ppermute | solution.py:306
  47.3 18.9 %collective-permute-start = (bf16[128,1152]{1,0:T(8,128)(2,1)S(1)}, bf16[128,1152]{1,0:T(8,128)(2,1)S(1)}, u32[]{:S(2)}, u32[]{:S(2)}) collective-permute-start(bf16[128,1152]{1,0:T(8,128)(2,1)S(1)} %assemble.1.refs_0_.block_ref), channel_id=1, source_target_pairs={{0,64},{32,96},{64,128},{96,160},{128,192},{160,224},{192,256},{22... | collective-permute-start | bytes 884744 | tf_op jit(solution)/shard_map/ppermute | solution.py:20
  52.0 33.0 %all-to-all-start.1 = ((bf16[32,54,128]{2,1,0:T(8,128)(2,1)}), bf16[32,54,128]{2,1,0:T(8,128)(2,1)S(1)}, u32[]{:S(2)}, u32[]{:S(2)}) async-start(bf16[32,54,128]{2,1,0:T(8,128)(2,1)} %send_back.1), calls=%async_computation.1 | async-start | bytes 917504 | tf_op jit(solution)/shard_map/all_to_all | solution.py:360
  66.3 18.7 %copy-start.1 = (s32[1,1,32,6]{2,1,3,0:T(1,128)S(1)}, s32[1,1,32,6]{2,1,3,0:T(1,128)}, u32[]{:S(2)}) copy-start(s32[1,1,32,6]{2,1,3,0:T(1,128)} %param.9) | copy-start | bytes 2308
  66.3 6.7 %collective-permute-start.1 = (bf16[128,1152]{1,0:T(8,128)(2,1)S(1)}, bf16[128,1152]{1,0:T(8,128)(2,1)S(1)}, u32[]{:S(2)}, u32[]{:S(2)}) collective-permute-start(bf16[128,1152]{1,0:T(8,128)(2,1)S(1)} %relay_blocks.1), channel_id=1, source_target_pairs={{0,32},{32,64},{64,96},{96,128},{128,160},{160,192},{192,224},{224... | collective-permute-start | bytes 884744 | tf_op jit(solution)/shard_map/ppermute | solution.py:20
  68.7 4.3 %collective-permute-start.2 = (bf16[128,1152]{1,0:T(8,128)(2,1)S(1)}, bf16[128,1152]{1,0:T(8,128)(2,1)S(1)}, u32[]{:S(2)}, u32[]{:S(2)}) collective-permute-start(bf16[128,1152]{1,0:T(8,128)(2,1)S(1)} %collective-permute-done.refs_1_), channel_id=1, source_target_pairs={{0,32},{32,0},{64,96},{96,64},{128,160},{160,128},{192,224},{224,1... | collective-permute-start | bytes 884744 | tf_op jit(solution)/shard_map/ppermute | solution.py:306

commit v6 on v5

--- a/solution.py
+++ b/solution.py
@@ -85,6 +85,14 @@
     rows = packet_ref.shape[0] - AUX_ROWS
     kept = packet_ref[rows:, 0:rows].astype(F32)
     return jnp.sum(jnp.where(iota(kept.shape, 0) == stop, kept, 0.0), axis=0, keepdims=True).astype(jnp.int32)
+
+
+def owned_rows(listed_ref, tally, group_at, width):
+    peers = tally.shape[0]
+    mine = jnp.sum(jnp.where(iota(tally.shape, 0) == group_at, tally, 0), axis=0, keepdims=True)
+    diagonal = iota((peers, peers), 0) == iota((peers, peers), 1)
+    outgoing = jnp.sum(jnp.where(diagonal, mine, 0), axis=1, keepdims=True)
+    return hits([jnp.where(outgoing > slot, rows, -1) for slot, rows in enumerate(upright(listed_ref))], width)
 
 
 def slopes_for(text, image, places, scale, shift):
@@ -158,10 +166,11 @@
         out_ref[...] = own_ref[...]
 
 
-def assemble_kernel(chunks_ref, tally_ref, block_ref, staging, rows_ref):
+def assemble_kernel(chunks_ref, tally_ref, block_ref, places_ref, staging, rows_ref):
     slot_cap = rows_ref.shape[0] // chunks_ref.shape[0]
     chunks_to_rows(chunks_ref, staging, rows_ref)
     places = block_places(tally_ref[0], lax.axis_index("grp"), slot_cap, block_ref.shape[0])
+    places_ref[...] = places
     block_ref[...] = lax.dot_general(
         places, rows_ref[...], (((0,), (0,)), ((), ())), preferred_element_type=F32
     ).astype(BF16)
@@ -185,11 +194,8 @@
         grad_ref[:, start : start + WIDTH] = total.astype(BF16)
 
 
-def send_kernel(tally_ref, grad_ref, chunks_hbm, staging, chunks_ref, sent):
-    rows, width = grad_ref.shape
-    slot_cap = chunks_ref.shape[1] * LANES // width
-    slots = block_places(tally_ref[0], lax.axis_index("grp"), slot_cap, rows)
-    gathered = jnp.dot(slots, grad_ref[...], preferred_element_type=F32)
+def send_kernel(places_ref, grad_ref, chunks_hbm, staging, chunks_ref, sent):
+    gathered = jnp.dot(places_ref[...], grad_ref[...], preferred_element_type=F32)
     for copy in rows_to_chunks(gathered, staging, chunks_ref, chunks_hbm, sent):
         copy.wait()
 
@@ -203,8 +209,9 @@
     ]
 
 
-def image_kernel(scale_ref, shift_ref, packet_ref, *refs):
-    blocks, grad_hbm, grad_ref, sent = refs[:STOPS], *refs[STOPS:]
+def image_kernel(scale_ref, shift_ref, listed_ref, tally_ref, packet_ref, *refs):
+    blocks, grad_hbm, owned_ref, grad_ref, sent = refs[:STOPS], *refs[STOPS:]
+    owned_ref[...] = owned_rows(listed_ref, tally_ref[0], lax.axis_index("grp"), owned_ref.shape[1])
     scale, shift = scale_ref[0], shift_ref[0]
     rows = grad_ref.shape[0]
     image = packet_ref[0:rows, :]
@@ -226,16 +233,9 @@
         copy.wait()
 
 
-def return_kernel(chunks_ref, listed_ref, tally_ref, grad_hbm, staging, rows_ref, grad_ref, sent):
+def return_kernel(chunks_ref, owned_ref, grad_hbm, staging, rows_ref, grad_ref, sent):
     chunks_to_rows(chunks_ref, staging, rows_ref)
-    tally = tally_ref[0]
-    peers = tally.shape[0]
-    mine = jnp.sum(jnp.where(iota(tally.shape, 0) == lax.axis_index("grp"), tally, 0), axis=0, keepdims=True)
-    diagonal = iota((peers, peers), 0) == iota((peers, peers), 1)
-    outgoing = jnp.sum(jnp.where(diagonal, mine, 0), axis=1, keepdims=True)
-    owned = hits(
-        [jnp.where(outgoing > slot, rows, -1) for slot, rows in enumerate(upright(listed_ref))], grad_ref.shape[0]
-    )
+    owned = owned_ref[...]
     copies = column_copies(grad_ref, grad_hbm, sent)
     for part, copy in enumerate(copies):
         columns = slice(part * WIDTH, (part + 1) * WIDTH)
@@ -340,9 +340,10 @@
     relayed = call(keep_even, [whole] * 2, in_vmem(packet_shape), name="relay_images")(packet, packet_two)
     packet_relay = passed_along(relayed, "loop", -1)
 
-    block = call(assemble_kernel, [whole] * 2, in_vmem(block_shape), [staging, slot_rows], name="assemble")(
-        incoming, sent_tally
-    )
+    slot_shape = jax.ShapeDtypeStruct((group_count * slot_cap, text_rows), BF16)
+    block, slot_places = call(
+        assemble_kernel, [whole] * 2, (in_vmem(block_shape), in_vmem(slot_shape)), [staging, slot_rows], name="assemble"
+    )(incoming, sent_tally)
 
     block_grad = call(text_kernel, [scalar] * 2 + [whole] * (1 + STOPS), in_vmem(block_shape), name="text_grads")(
         score_scale_factor, score_shift_term, block, packet, packet_two, packet_relay, packet_swap
@@ -356,7 +357,7 @@
         name="send_back",
         cost=huge,
         outs=remote,
-    )(sent_tally, block_grad)
+    )(slot_places, block_grad)
     returned = lax.all_to_all(sendback, "grp", split_axis=0, concat_axis=0, tiled=True)
 
     relayed_block = call(keep_odd, [whole] * 2, in_vmem(block_shape), name="relay_blocks", cost=huge)(
@@ -364,24 +365,24 @@
     )
     block_relay = passed_along(relayed_block, "loop", 1)
     block_swap = swapped(block_two)
-    image_grad = call(
+    image_grad, owned = call(
         image_kernel,
-        [scalar] * 2 + [whole] * (1 + STOPS),
-        jax.ShapeDtypeStruct((image_rows, features), F32),
+        [scalar] * 2 + [whole] * (3 + STOPS),
+        (jax.ShapeDtypeStruct((image_rows, features), F32), in_vmem(slot_shape)),
         [pltpu.VMEM((image_rows, features), F32), column_sems],
         name="image_grads",
         cost=big,
-        outs=remote,
-    )(score_scale_factor, score_shift_term, packet, block, block_two, block_relay, block_swap)
+        outs=(remote, whole),
+    )(score_scale_factor, score_shift_term, listed, sent_tally, packet, block, block_two, block_relay, block_swap)
 
     text_grad = call(
         return_kernel,
-        [whole] * 3,
+        [whole] * 2,
         jax.ShapeDtypeStruct((text_rows, features), F32),
         [staging, slot_rows, pltpu.VMEM((text_rows, features), F32), column_sems],
         name="give_back",
         outs=remote,
-    )(returned, listed, sent_tally)
+    )(returned, owned)
     return (image_grad, text_grad)
 
 

time: 86.8 us -> 86.5 us (level)
  no operation moved by 1% of the time
where the time goes in v6:
time: 86.5 us; the launch traced here: 86 us
  starting transfers between devices  49.4 us (57%)
  waiting for transfers between devices  24.5 us (28%)
  Pallas kernels  9.97 us (12%)
  between operations  2.08 us (2%)
    all_to_all x1, starting transfers between devices, local(): lax.all_to_all(outgoing, 'grp', split_axis=0, concat_axis=0, tiled=True)  20.6 us
    all_to_all x1, starting transfers between devices, local(): lax.all_to_all(sendback, 'grp', split_axis=0, concat_axis=0, tiled=True)  14.2 us
    all_to_all x1, waiting for transfers between devices, local(): lax.all_to_all(outgoing, 'grp', split_axis=0, concat_axis=0, tiled=True)  12.6 us
    ppermute x4, starting transfers between devices, passed_along(): return lax.ppermute(value, axis, pairs)  10.7 us
    all_to_all x1, waiting for transfers between devices, local(): lax.all_to_all(sendback, 'grp', split_axis=0, concat_axis=0, tiled=True)  9.54 us
    ppermute x2, starting transfers between devices, swapped(): lax.ppermute(value, 'loop', [(source, source ^ 1) for source in range(loo...  3.91 us
    pallas_call x1, Pallas kernels, local(): call(image_kernel, [scalar] * 2 + [whole] * (3 + STOPS), (jax.ShapeDtypeS...  2.47 us
    ppermute x4, waiting for transfers between devices, passed_along(): return lax.ppermute(value, axis, pairs)  2.37 us
  transfers between devices with their start and end apart: 8, of which 3 were waited for; matrix products, arithmetic and copies ran while one was open for 0% of the time, Pallas kernels for 8%

profile of v6, /device:TPU:159, one launch (start us, length us, event | category | flops | bytes accessed | tf_op | source)
XLA Modules:
  0.0 86.0 jit_solution(14280396432562788497)
XLA Ops:
  0.6 2.2 %prepare.1 = (bf16[272,1152]{1,0:T(8,128)(2,1)S(1)}, bf16[32,54,128]{2,1,0:T(8,128)(2,1)}) custom-call(f32[256,1152]{1,0:T(8,128)} %refs_0_.1, s32[1,256]{1,0:T(1,128)} %bitcast.6, f32[128,1152]{1,0:T(8,128)} %refs_2_.1, s32[6,1,32]{2,1,0:T(1,128)} %bitcast.4), custom_call_target="tpu_custom_call" | custom-call | tf_op jit(solution)/shard_map/prepare/pallas_call | solution.py:309
  2.9 3.1 %collective-permute-start.3 = (bf16[272,1152]{1,0:T(8,128)(2,1)S(1)}, bf16[272,1152]{1,0:T(8,128)(2,1)S(1)}, u32[]{:S(2)}, u32[]{:S(2)}) collective-permute-start(bf16[272,1152]{1,0:T(8,128)(2,1)S(1)} %get-tuple-element.8.packet_ref.refs_0_), channel_id=1, source_target_pairs={{0,960},{32,992},{64,0},{96,32},{128,64},{160,96},{192,128},{224,1... | collective-permute-start | bytes 1880072 | tf_op jit(solution)/shard_map/ppermute | solution.py:20
  5.9 0.0 copy-start
  5.9 20.6 %all-to-all-start = ((bf16[32,54,128]{2,1,0:T(8,128)(2,1)}), bf16[32,54,128]{2,1,0:T(8,128)(2,1)S(1)}, u32[]{:S(2)}, u32[]{:S(2)}) async-start(bf16[32,54,128]{2,1,0:T(8,128)(2,1)} %get-tuple-element.9), calls=%async_computation | async-start | bytes 917504 | tf_op jit(solution)/shard_map/all_to_all | solution.py:338
  26.5 0.0 collective-permute-done.3.refs_1_
  26.5 0.9 %relay_images.1 = bf16[272,1152]{1,0:T(8,128)(2,1)} custom-call(bf16[272,1152]{1,0:T(8,128)(2,1)S(1)} %get-tuple-element.8.packet_ref.refs_0_, bf16[272,1152]{1,0:T(8,128)(2,1)S(1)} %collective-permute-done.3.refs_1_), custom_call_target="tpu_custom_call" | custom-call | tf_op jit(solution)/shard_map/relay_images/pallas_call | solution.py:340
  27.4 3.4 %collective-permute-start.4 = (bf16[272,1152]{1,0:T(8,128)(2,1)}, bf16[272,1152]{1,0:T(8,128)(2,1)S(1)}, u32[]{:S(2)}, u32[]{:S(2)}) collective-permute-start(bf16[272,1152]{1,0:T(8,128)(2,1)} %relay_images.1), channel_id=1, source_target_pairs={{0,992},{32,0},{64,32},{96,64},{128,96},{160,128},{192,160},{224,1... | collective-permute-start | bytes 1880072 | tf_op jit(solution)/shard_map/ppermute | solution.py:20
  30.8 1.9 %collective-permute-start.5 = (bf16[272,1152]{1,0:T(8,128)(2,1)S(1)}, bf16[272,1152]{1,0:T(8,128)(2,1)S(1)}, u32[]{:S(2)}, u32[]{:S(2)}) collective-permute-start(bf16[272,1152]{1,0:T(8,128)(2,1)S(1)} %collective-permute-done.3.refs_1_), channel_id=1, source_target_pairs={{0,32},{32,0},{64,96},{96,64},{128,160},{160,128},{192,224},{224,1... | collective-permute-start | bytes 1880072 | tf_op jit(solution)/shard_map/ppermute | solution.py:306
  34.1 12.6 %all-to-all-done.chunks_ref = bf16[32,54,128]{2,1,0:T(8,128)(2,1)S(1)} async-done(((bf16[32,54,128]{2,1,0:T(8,128)(2,1)}), bf16[32,54,128]{2,1,0:T(8,128)(2,1)S(1)}, u32[]{:S(2)}, u32[]{:S(2)}) %all-to-all-start) | async-done | bytes 442400 | tf_op jit(solution)/shard_map/all_to_all | solution.py:338
  46.7 0.0 copy-done
  46.7 0.6 assemble.1
  47.3 1.9 %collective-permute-start = (bf16[128,1152]{1,0:T(8,128)(2,1)S(1)}, bf16[128,1152]{1,0:T(8,128)(2,1)S(1)}, u32[]{:S(2)}, u32[]{:S(2)}) collective-permute-start(bf16[128,1152]{1,0:T(8,128)(2,1)S(1)} %get-tuple-element.10.refs_0_.block_ref), channel_id=1, source_target_pairs={{0,64},{32,96},{64,128},{96,160},{128,192},{160,224},{192,256},{22... | collective-permute-start | bytes 884744 | tf_op jit(solution)/shard_map/ppermute | solution.py:20
  49.2 0.0 collective-permute-done.4.refs_2_
  49.2 0.0 collective-permute-done.5.refs_3_
  49.2 1.4 %text_grads.1.grad_ref = bf16[128,1152]{1,0:T(8,128)(2,1)S(1)} custom-call(f32[1]{0:T(128)S(6)} %copy.9.scale_ref, f32[1]{0:T(128)S(6)} %copy.10.shift_ref, bf16[128,1152]{1,0:T(8,128)(2,1)S(1)} %get-tuple-element.10.refs_0_.block_ref, bf16[272,1152]{1,0:T(8,128)(2,1)S(1)} %get-tuple-element.8.packet_ref.refs_0_, ...), custom_call_target="tpu_custom_call" | custom-call | tf_op jit(solution)/shard_map/text_grads/pallas_call | solution.py:348
  50.7 1.1 %send_back.1 = bf16[32,54,128]{2,1,0:T(8,128)(2,1)} custom-call(bf16[192,128]{1,0:T(8,128)(2,1)S(1)} %get-tuple-element.12.places_ref, bf16[128,1152]{1,0:T(8,128)(2,1)S(1)} %text_grads.1.grad_ref), custom_call_target="tpu_custom_call" | custom-call | flops 49999998976 | tf_op jit(solution)/shard_map/send_back/pallas_call | solution.py:352
  51.8 14.2 %all-to-all-start.1 = ((bf16[32,54,128]{2,1,0:T(8,128)(2,1)}), bf16[32,54,128]{2,1,0:T(8,128)(2,1)S(1)}, u32[]{:S(2)}, u32[]{:S(2)}) async-start(bf16[32,54,128]{2,1,0:T(8,128)(2,1)} %send_back.1), calls=%async_computation.1 | async-start | bytes 917504 | tf_op jit(solution)/shard_map/all_to_all | solution.py:361
  66.0 0.0 copy-start.1
  66.0 0.0 collective-permute-done.refs_1_
  66.1 2.4 %collective-permute-start.1 = (bf16[128,1152]{1,0:T(8,128)(2,1)S(1)}, bf16[128,1152]{1,0:T(8,128)(2,1)S(1)}, u32[]{:S(2)}, u32[]{:S(2)}) collective-permute-start(bf16[128,1152]{1,0:T(8,128)(2,1)S(1)} %relay_blocks.1), channel_id=1, source_target_pairs={{0,32},{32,64},{64,96},{96,128},{128,160},{160,192},{192,224},{224... | collective-permute-start | bytes 884744 | tf_op jit(solution)/shard_map/ppermute | solution.py:20
  68.4 2.0 %collective-permute-start.2 = (bf16[128,1152]{1,0:T(8,128)(2,1)S(1)}, bf16[128,1152]{1,0:T(8,128)(2,1)S(1)}, u32[]{:S(2)}, u32[]{:S(2)}) collective-permute-start(bf16[128,1152]{1,0:T(8,128)(2,1)S(1)} %collective-permute-done.refs_1_), channel_id=1, source_target_pairs={{0,32},{32,0},{64,96},{96,64},{128,160},{160,128},{192,224},{224,1... | collective-permute-start | bytes 884744 | tf_op jit(solution)/shard_map/ppermute | solution.py:306
  70.4 2.4 %collective-permute-done.1.refs_2_ = bf16[128,1152]{1,0:T(8,128)(2,1)S(1)} collective-permute-done((bf16[128,1152]{1,0:T(8,128)(2,1)S(1)}, bf16[128,1152]{1,0:T(8,128)(2,1)S(1)}, u32[]{:S(2)}, u32[]{:S(2)}) %collective-permute-start.1) | collective-permute-done | bytes 294944 | tf_op jit(solution)/shard_map/ppermute | solution.py:20
  72.8 0.0 collective-permute-done.2.refs_3_
  72.8 0.0 copy-done.1
  72.8 2.5 %image_grads.1 = (f32[256,1152]{1,0:T(8,128)}, bf16[192,128]{1,0:T(8,128)(2,1)S(1)}) custom-call(f32[1]{0:T(128)S(6)} %copy.9.scale_ref, f32[1]{0:T(128)S(6)} %copy.10.shift_ref, s32[6,1,32]{2,1,0:T(1,128)S(1)} %bitcast.5, s32[1,32,32]{2,1,0:T(8,128)S(1)} %copy-done, bf16[272,1152]{1,0:T(8,128)(2,1)S(1)} %get-tuple-element.8.packet_ref.refs_0_, ...), custom_call_target="tpu_custom_call" | custom-call | flops 905969664 | bytes 2359296 | tf_op jit(solution)/shard_map/image_grads/pallas_call | solution.py:368
  75.3 9.5 %all-to-all-done.1.chunks_ref = bf16[32,54,128]{2,1,0:T(8,128)(2,1)S(1)} async-done(((bf16[32,54,128]{2,1,0:T(8,128)(2,1)}), bf16[32,54,128]{2,1,0:T(8,128)(2,1)S(1)}, u32[]{:S(2)}, u32[]{:S(2)}) %all-to-all-start.1) | async-done | bytes 442400 | tf_op jit(solution)/shard_map/all_to_all | solution.py:361
  84.8 1.2 %give_back.1 = f32[128,1152]{1,0:T(8,128)} custom-call(bf16[32,54,128]{2,1,0:T(8,128)(2,1)S(1)} %all-to-all-done.1.chunks_ref, bf16[192,128]{1,0:T(8,128)(2,1)S(1)} %get-tuple-element.13.owned_ref), custom_call_target="tpu_custom_call" | custom-call | tf_op jit(solution)/shard_map/give_back/pallas_call | solution.py:378
  (1 shorter events, 0.0 us)
Async XLA Ops:
  2.9 23.7 %collective-permute-start.3 = (bf16[272,1152]{1,0:T(8,128)(2,1)S(1)}, bf16[272,1152]{1,0:T(8,128)(2,1)S(1)}, u32[]{:S(2)}, u32[]{:S(2)}) collective-permute-start(bf16[272,1152]{1,0:T(8,128)(2,1)S(1)} %get-tuple-element.8.packet_ref.refs_0_), channel_id=1, source_target_pairs={{0,960},{32,992},{64,0},{96,32},{128,64},{160,96},{192,128},{224,1... | collective-permute-start | bytes 1880072 | tf_op jit(solution)/shard_map/ppermute | solution.py:20
  5.9 40.8 %copy-start = (s32[1,32,32]{2,1,0:T(8,128)S(1)}, s32[1,32,32]{2,1,0:T(8,128)}, u32[]{:S(2)}) copy-start(s32[1,32,32]{2,1,0:T(8,128)} %tally_ref.3) | copy-start | bytes 12292
  5.9 40.7 %all-to-all-start = ((bf16[32,54,128]{2,1,0:T(8,128)(2,1)}), bf16[32,54,128]{2,1,0:T(8,128)(2,1)S(1)}, u32[]{:S(2)}, u32[]{:S(2)}) async-start(bf16[32,54,128]{2,1,0:T(8,128)(2,1)} %get-tuple-element.9), calls=%async_computation | async-start | bytes 917504 | tf_op jit(solution)/shard_map/all_to_all | solution.py:338
  27.4 21.8 %collective-permute-start.4 = (bf16[272,1152]{1,0:T(8,128)(2,1)}, bf16[272,1152]{1,0:T(8,128)(2,1)S(1)}, u32[]{:S(2)}, u32[]{:S(2)}) collective-permute-start(bf16[272,1152]{1,0:T(8,128)(2,1)} %relay_images.1), channel_id=1, source_target_pairs={{0,992},{32,0},{64,32},{96,64},{128,96},{160,128},{192,160},{224,1... | collective-permute-start | bytes 1880072 | tf_op jit(solution)/shard_map/ppermute | solution.py:20
  30.8 18.4 %collective-permute-start.5 = (bf16[272,1152]{1,0:T(8,128)(2,1)S(1)}, bf16[272,1152]{1,0:T(8,128)(2,1)S(1)}, u32[]{:S(2)}, u32[]{:S(2)}) collective-permute-start(bf16[272,1152]{1,0:T(8,128)(2,1)S(1)} %collective-permute-done.3.refs_1_), channel_id=1, source_target_pairs={{0,32},{32,0},{64,96},{96,64},{128,160},{160,128},{192,224},{224,1... | collective-permute-start | bytes 1880072 | tf_op jit(solution)/shard_map/ppermute | solution.py:306
  47.3 18.7 %collective-permute-start = (bf16[128,1152]{1,0:T(8,128)(2,1)S(1)}, bf16[128,1152]{1,0:T(8,128)(2,1)S(1)}, u32[]{:S(2)}, u32[]{:S(2)}) collective-permute-start(bf16[128,1152]{1,0:T(8,128)(2,1)S(1)} %get-tuple-element.10.refs_0_.block_ref), channel_id=1, source_target_pairs={{0,64},{32,96},{64,128},{96,160},{128,192},{160,224},{192,256},{22... | collective-permute-start | bytes 884744 | tf_op jit(solution)/shard_map/ppermute | solution.py:20
  51.8 33.0 %all-to-all-start.1 = ((bf16[32,54,128]{2,1,0:T(8,128)(2,1)}), bf16[32,54,128]{2,1,0:T(8,128)(2,1)S(1)}, u32[]{:S(2)}, u32[]{:S(2)}) async-start(bf16[32,54,128]{2,1,0:T(8,128)(2,1)} %send_back.1), calls=%async_computation.1 | async-start | bytes 917504 | tf_op jit(solution)/shard_map/all_to_all | solution.py:361
  66.0 6.8 %copy-start.1 = (s32[1,1,32,6]{2,1,3,0:T(1,128)S(1)}, s32[1,1,32,6]{2,1,3,0:T(1,128)}, u32[]{:S(2)}) copy-start(s32[1,1,32,6]{2,1,3,0:T(1,128)} %param.9) | copy-start | bytes 2308
  66.1 6.7 %collective-permute-start.1 = (bf16[128,1152]{1,0:T(8,128)(2,1)S(1)}, bf16[128,1152]{1,0:T(8,128)(2,1)S(1)}, u32[]{:S(2)}, u32[]{:S(2)}) collective-permute-start(bf16[128,1152]{1,0:T(8,128)(2,1)S(1)} %relay_blocks.1), channel_id=1, source_target_pairs={{0,32},{32,64},{64,96},{96,128},{128,160},{160,192},{192,224},{224... | collective-permute-start | bytes 884744 | tf_op jit(solution)/shard_map/ppermute | solution.py:20
  68.4 4.3 %collective-permute-start.2 = (bf16[128,1152]{1,0:T(8,128)(2,1)S(1)}, bf16[128,1152]{1,0:T(8,128)(2,1)S(1)}, u32[]{:S(2)}, u32[]{:S(2)}) collective-permute-start(bf16[128,1152]{1,0:T(8,128)(2,1)S(1)} %collective-permute-done.refs_1_), channel_id=1, source_target_pairs={{0,32},{32,0},{64,96},{96,64},{128,160},{160,128},{192,224},{224,1... | collective-permute-start | bytes 884744 | tf_op jit(solution)/shard_map/ppermute | solution.py:306

commit v7 on v6

--- a/solution.py
+++ b/solution.py
@@ -8,7 +8,7 @@
 STOPS = 4
 LANES = 128
 AUX_ROWS = 16
-PARTS = 4
+PARTS = 2
 WIDTH = 3 * LANES
 BF16 = jnp.bfloat16
 F32 = jnp.float32

time: 86.5 us -> 86.5 us (level)
  no operation moved by 1% of the time
where the time goes in v7:
time: 86.5 us; the launch traced here: 86 us
  starting transfers between devices  49.4 us (57%)
  waiting for transfers between devices  24.5 us (28%)
  Pallas kernels  9.97 us (12%)
  between operations  2.08 us (2%)
    all_to_all x1, starting transfers between devices, local(): lax.all_to_all(outgoing, 'grp', split_axis=0, concat_axis=0, tiled=True)  20.6 us
    all_to_all x1, starting transfers between devices, local(): lax.all_to_all(sendback, 'grp', split_axis=0, concat_axis=0, tiled=True)  14.2 us
    all_to_all x1, waiting for transfers between devices, local(): lax.all_to_all(outgoing, 'grp', split_axis=0, concat_axis=0, tiled=True)  12.6 us
    ppermute x4, starting transfers between devices, passed_along(): return lax.ppermute(value, axis, pairs)  10.7 us
    all_to_all x1, waiting for transfers between devices, local(): lax.all_to_all(sendback, 'grp', split_axis=0, concat_axis=0, tiled=True)  9.52 us
    ppermute x2, starting transfers between devices, swapped(): lax.ppermute(value, 'loop', [(source, source ^ 1) for source in range(loo...  3.92 us
    pallas_call x1, Pallas kernels, local(): call(image_kernel, [scalar] * 2 + [whole] * (3 + STOPS), (jax.ShapeDtypeS...  2.47 us
    ppermute x4, waiting for transfers between devices, passed_along(): return lax.ppermute(value, axis, pairs)  2.37 us
  transfers between devices with their start and end apart: 8, of which 3 were waited for; matrix products, arithmetic and copies ran while one was open for 0% of the time, Pallas kernels for 8%

profile of v7, /device:TPU:159, one launch (start us, length us, event | category | flops | bytes accessed | tf_op | source)
XLA Modules:
  0.0 86.0 jit_solution(11026035937801149633)
XLA Ops:
  0.6 2.2 %prepare.1 = (bf16[272,1152]{1,0:T(8,128)(2,1)S(1)}, bf16[32,54,128]{2,1,0:T(8,128)(2,1)}) custom-call(f32[256,1152]{1,0:T(8,128)} %refs_0_.1, s32[1,256]{1,0:T(1,128)} %bitcast.6, f32[128,1152]{1,0:T(8,128)} %refs_2_.1, s32[6,1,32]{2,1,0:T(1,128)} %bitcast.4), custom_call_target="tpu_custom_call" | custom-call | tf_op jit(solution)/shard_map/prepare/pallas_call | solution.py:309
  2.9 3.1 %collective-permute-start.3 = (bf16[272,1152]{1,0:T(8,128)(2,1)S(1)}, bf16[272,1152]{1,0:T(8,128)(2,1)S(1)}, u32[]{:S(2)}, u32[]{:S(2)}) collective-permute-start(bf16[272,1152]{1,0:T(8,128)(2,1)S(1)} %get-tuple-element.8.packet_ref.refs_0_), channel_id=1, source_target_pairs={{0,960},{32,992},{64,0},{96,32},{128,64},{160,96},{192,128},{224,1... | collective-permute-start | bytes 1880072 | tf_op jit(solution)/shard_map/ppermute | solution.py:20
  5.9 0.0 copy-start
  5.9 20.6 %all-to-all-start = ((bf16[32,54,128]{2,1,0:T(8,128)(2,1)}), bf16[32,54,128]{2,1,0:T(8,128)(2,1)S(1)}, u32[]{:S(2)}, u32[]{:S(2)}) async-start(bf16[32,54,128]{2,1,0:T(8,128)(2,1)} %get-tuple-element.9), calls=%async_computation | async-start | bytes 917504 | tf_op jit(solution)/shard_map/all_to_all | solution.py:338
  26.5 0.0 collective-permute-done.3.refs_1_
  26.5 0.9 %relay_images.1 = bf16[272,1152]{1,0:T(8,128)(2,1)} custom-call(bf16[272,1152]{1,0:T(8,128)(2,1)S(1)} %get-tuple-element.8.packet_ref.refs_0_, bf16[272,1152]{1,0:T(8,128)(2,1)S(1)} %collective-permute-done.3.refs_1_), custom_call_target="tpu_custom_call" | custom-call | tf_op jit(solution)/shard_map/relay_images/pallas_call | solution.py:340
  27.4 3.4 %collective-permute-start.4 = (bf16[272,1152]{1,0:T(8,128)(2,1)}, bf16[272,1152]{1,0:T(8,128)(2,1)S(1)}, u32[]{:S(2)}, u32[]{:S(2)}) collective-permute-start(bf16[272,1152]{1,0:T(8,128)(2,1)} %relay_images.1), channel_id=1, source_target_pairs={{0,992},{32,0},{64,32},{96,64},{128,96},{160,128},{192,160},{224,1... | collective-permute-start | bytes 1880072 | tf_op jit(solution)/shard_map/ppermute | solution.py:20
  30.8 1.9 %collective-permute-start.5 = (bf16[272,1152]{1,0:T(8,128)(2,1)S(1)}, bf16[272,1152]{1,0:T(8,128)(2,1)S(1)}, u32[]{:S(2)}, u32[]{:S(2)}) collective-permute-start(bf16[272,1152]{1,0:T(8,128)(2,1)S(1)} %collective-permute-done.3.refs_1_), channel_id=1, source_target_pairs={{0,32},{32,0},{64,96},{96,64},{128,160},{160,128},{192,224},{224,1... | collective-permute-start | bytes 1880072 | tf_op jit(solution)/shard_map/ppermute | solution.py:306
  34.1 12.6 %all-to-all-done.chunks_ref = bf16[32,54,128]{2,1,0:T(8,128)(2,1)S(1)} async-done(((bf16[32,54,128]{2,1,0:T(8,128)(2,1)}), bf16[32,54,128]{2,1,0:T(8,128)(2,1)S(1)}, u32[]{:S(2)}, u32[]{:S(2)}) %all-to-all-start) | async-done | bytes 442400 | tf_op jit(solution)/shard_map/all_to_all | solution.py:338
  46.7 0.0 copy-done
  46.7 0.6 assemble.1
  47.3 1.9 %collective-permute-start = (bf16[128,1152]{1,0:T(8,128)(2,1)S(1)}, bf16[128,1152]{1,0:T(8,128)(2,1)S(1)}, u32[]{:S(2)}, u32[]{:S(2)}) collective-permute-start(bf16[128,1152]{1,0:T(8,128)(2,1)S(1)} %get-tuple-element.10.refs_0_.block_ref), channel_id=1, source_target_pairs={{0,64},{32,96},{64,128},{96,160},{128,192},{160,224},{192,256},{22... | collective-permute-start | bytes 884744 | tf_op jit(solution)/shard_map/ppermute | solution.py:20
  49.2 0.0 collective-permute-done.4.refs_2_
  49.2 0.0 collective-permute-done.5.refs_3_
  49.2 1.4 %text_grads.1.grad_ref = bf16[128,1152]{1,0:T(8,128)(2,1)S(1)} custom-call(f32[1]{0:T(128)S(6)} %copy.9.scale_ref, f32[1]{0:T(128)S(6)} %copy.10.shift_ref, bf16[128,1152]{1,0:T(8,128)(2,1)S(1)} %get-tuple-element.10.refs_0_.block_ref, bf16[272,1152]{1,0:T(8,128)(2,1)S(1)} %get-tuple-element.8.packet_ref.refs_0_, ...), custom_call_target="tpu_custom_call" | custom-call | tf_op jit(solution)/shard_map/text_grads/pallas_call | solution.py:348
  50.7 1.1 %send_back.1 = bf16[32,54,128]{2,1,0:T(8,128)(2,1)} custom-call(bf16[192,128]{1,0:T(8,128)(2,1)S(1)} %get-tuple-element.12.places_ref, bf16[128,1152]{1,0:T(8,128)(2,1)S(1)} %text_grads.1.grad_ref), custom_call_target="tpu_custom_call" | custom-call | flops 49999998976 | tf_op jit(solution)/shard_map/send_back/pallas_call | solution.py:352
  51.8 14.2 %all-to-all-start.1 = ((bf16[32,54,128]{2,1,0:T(8,128)(2,1)}), bf16[32,54,128]{2,1,0:T(8,128)(2,1)S(1)}, u32[]{:S(2)}, u32[]{:S(2)}) async-start(bf16[32,54,128]{2,1,0:T(8,128)(2,1)} %send_back.1), calls=%async_computation.1 | async-start | bytes 917504 | tf_op jit(solution)/shard_map/all_to_all | solution.py:361
  66.0 0.0 copy-start.1
  66.0 0.0 collective-permute-done.refs_1_
  66.1 2.4 %collective-permute-start.1 = (bf16[128,1152]{1,0:T(8,128)(2,1)S(1)}, bf16[128,1152]{1,0:T(8,128)(2,1)S(1)}, u32[]{:S(2)}, u32[]{:S(2)}) collective-permute-start(bf16[128,1152]{1,0:T(8,128)(2,1)S(1)} %relay_blocks.1), channel_id=1, source_target_pairs={{0,32},{32,64},{64,96},{96,128},{128,160},{160,192},{192,224},{224... | collective-permute-start | bytes 884744 | tf_op jit(solution)/shard_map/ppermute | solution.py:20
  68.4 2.0 %collective-permute-start.2 = (bf16[128,1152]{1,0:T(8,128)(2,1)S(1)}, bf16[128,1152]{1,0:T(8,128)(2,1)S(1)}, u32[]{:S(2)}, u32[]{:S(2)}) collective-permute-start(bf16[128,1152]{1,0:T(8,128)(2,1)S(1)} %collective-permute-done.refs_1_), channel_id=1, source_target_pairs={{0,32},{32,0},{64,96},{96,64},{128,160},{160,128},{192,224},{224,1... | collective-permute-start | bytes 884744 | tf_op jit(solution)/shard_map/ppermute | solution.py:306
  70.4 2.4 %collective-permute-done.1.refs_2_ = bf16[128,1152]{1,0:T(8,128)(2,1)S(1)} collective-permute-done((bf16[128,1152]{1,0:T(8,128)(2,1)S(1)}, bf16[128,1152]{1,0:T(8,128)(2,1)S(1)}, u32[]{:S(2)}, u32[]{:S(2)}) %collective-permute-start.1) | collective-permute-done | bytes 294944 | tf_op jit(solution)/shard_map/ppermute | solution.py:20
  72.8 0.0 collective-permute-done.2.refs_3_
  72.8 0.0 copy-done.1
  72.8 2.5 %image_grads.1 = (f32[256,1152]{1,0:T(8,128)}, bf16[192,128]{1,0:T(8,128)(2,1)S(1)}) custom-call(f32[1]{0:T(128)S(6)} %copy.9.scale_ref, f32[1]{0:T(128)S(6)} %copy.10.shift_ref, s32[6,1,32]{2,1,0:T(1,128)S(1)} %bitcast.5, s32[1,32,32]{2,1,0:T(8,128)S(1)} %copy-done, bf16[272,1152]{1,0:T(8,128)(2,1)S(1)} %get-tuple-element.8.packet_ref.refs_0_, ...), custom_call_target="tpu_custom_call" | custom-call | flops 905969664 | bytes 2359296 | tf_op jit(solution)/shard_map/image_grads/pallas_call | solution.py:368
  75.3 9.5 %all-to-all-done.1.chunks_ref = bf16[32,54,128]{2,1,0:T(8,128)(2,1)S(1)} async-done(((bf16[32,54,128]{2,1,0:T(8,128)(2,1)}), bf16[32,54,128]{2,1,0:T(8,128)(2,1)S(1)}, u32[]{:S(2)}, u32[]{:S(2)}) %all-to-all-start.1) | async-done | bytes 442400 | tf_op jit(solution)/shard_map/all_to_all | solution.py:361
  84.8 1.2 %give_back.1 = f32[128,1152]{1,0:T(8,128)} custom-call(bf16[32,54,128]{2,1,0:T(8,128)(2,1)S(1)} %all-to-all-done.1.chunks_ref, bf16[192,128]{1,0:T(8,128)(2,1)S(1)} %get-tuple-element.13.owned_ref), custom_call_target="tpu_custom_call" | custom-call | tf_op jit(solution)/shard_map/give_back/pallas_call | solution.py:378
  (1 shorter events, 0.0 us)
Async XLA Ops:
  2.9 23.7 %collective-permute-start.3 = (bf16[272,1152]{1,0:T(8,128)(2,1)S(1)}, bf16[272,1152]{1,0:T(8,128)(2,1)S(1)}, u32[]{:S(2)}, u32[]{:S(2)}) collective-permute-start(bf16[272,1152]{1,0:T(8,128)(2,1)S(1)} %get-tuple-element.8.packet_ref.refs_0_), channel_id=1, source_target_pairs={{0,960},{32,992},{64,0},{96,32},{128,64},{160,96},{192,128},{224,1... | collective-permute-start | bytes 1880072 | tf_op jit(solution)/shard_map/ppermute | solution.py:20
  5.9 40.8 %copy-start = (s32[1,32,32]{2,1,0:T(8,128)S(1)}, s32[1,32,32]{2,1,0:T(8,128)}, u32[]{:S(2)}) copy-start(s32[1,32,32]{2,1,0:T(8,128)} %tally_ref.3) | copy-start | bytes 12292
  5.9 40.7 %all-to-all-start = ((bf16[32,54,128]{2,1,0:T(8,128)(2,1)}), bf16[32,54,128]{2,1,0:T(8,128)(2,1)S(1)}, u32[]{:S(2)}, u32[]{:S(2)}) async-start(bf16[32,54,128]{2,1,0:T(8,128)(2,1)} %get-tuple-element.9), calls=%async_computation | async-start | bytes 917504 | tf_op jit(solution)/shard_map/all_to_all | solution.py:338
  27.4 21.8 %collective-permute-start.4 = (bf16[272,1152]{1,0:T(8,128)(2,1)}, bf16[272,1152]{1,0:T(8,128)(2,1)S(1)}, u32[]{:S(2)}, u32[]{:S(2)}) collective-permute-start(bf16[272,1152]{1,0:T(8,128)(2,1)} %relay_images.1), channel_id=1, source_target_pairs={{0,992},{32,0},{64,32},{96,64},{128,96},{160,128},{192,160},{224,1... | collective-permute-start | bytes 1880072 | tf_op jit(solution)/shard_map/ppermute | solution.py:20
  30.8 18.4 %collective-permute-start.5 = (bf16[272,1152]{1,0:T(8,128)(2,1)S(1)}, bf16[272,1152]{1,0:T(8,128)(2,1)S(1)}, u32[]{:S(2)}, u32[]{:S(2)}) collective-permute-start(bf16[272,1152]{1,0:T(8,128)(2,1)S(1)} %collective-permute-done.3.refs_1_), channel_id=1, source_target_pairs={{0,32},{32,0},{64,96},{96,64},{128,160},{160,128},{192,224},{224,1... | collective-permute-start | bytes 1880072 | tf_op jit(solution)/shard_map/ppermute | solution.py:306
  47.3 18.7 %collective-permute-start = (bf16[128,1152]{1,0:T(8,128)(2,1)S(1)}, bf16[128,1152]{1,0:T(8,128)(2,1)S(1)}, u32[]{:S(2)}, u32[]{:S(2)}) collective-permute-start(bf16[128,1152]{1,0:T(8,128)(2,1)S(1)} %get-tuple-element.10.refs_0_.block_ref), channel_id=1, source_target_pairs={{0,64},{32,96},{64,128},{96,160},{128,192},{160,224},{192,256},{22... | collective-permute-start | bytes 884744 | tf_op jit(solution)/shard_map/ppermute | solution.py:20
  51.8 33.0 %all-to-all-start.1 = ((bf16[32,54,128]{2,1,0:T(8,128)(2,1)}), bf16[32,54,128]{2,1,0:T(8,128)(2,1)S(1)}, u32[]{:S(2)}, u32[]{:S(2)}) async-start(bf16[32,54,128]{2,1,0:T(8,128)(2,1)} %send_back.1), calls=%async_computation.1 | async-start | bytes 917504 | tf_op jit(solution)/shard_map/all_to_all | solution.py:361
  66.0 6.8 %copy-start.1 = (s32[1,1,32,6]{2,1,3,0:T(1,128)S(1)}, s32[1,1,32,6]{2,1,3,0:T(1,128)}, u32[]{:S(2)}) copy-start(s32[1,1,32,6]{2,1,3,0:T(1,128)} %param.9) | copy-start | bytes 2308
  66.1 6.7 %collective-permute-start.1 = (bf16[128,1152]{1,0:T(8,128)(2,1)S(1)}, bf16[128,1152]{1,0:T(8,128)(2,1)S(1)}, u32[]{:S(2)}, u32[]{:S(2)}) collective-permute-start(bf16[128,1152]{1,0:T(8,128)(2,1)S(1)} %relay_blocks.1), channel_id=1, source_target_pairs={{0,32},{32,64},{64,96},{96,128},{128,160},{160,192},{192,224},{224... | collective-permute-start | bytes 884744 | tf_op jit(solution)/shard_map/ppermute | solution.py:20
  68.4 4.4 %collective-permute-start.2 = (bf16[128,1152]{1,0:T(8,128)(2,1)S(1)}, bf16[128,1152]{1,0:T(8,128)(2,1)S(1)}, u32[]{:S(2)}, u32[]{:S(2)}) collective-permute-start(bf16[128,1152]{1,0:T(8,128)(2,1)S(1)} %collective-permute-done.refs_1_), channel_id=1, source_target_pairs={{0,32},{32,0},{64,96},{96,64},{128,160},{160,128},{192,224},{224,1... | collective-permute-start | bytes 884744 | tf_op jit(solution)/shard_map/ppermute | solution.py:306
